TPU v7x, 32 devices: a whole 2x2x4 slice. The times are simulated.
32 devices in a mesh: row: 8 (over z, core), col: 4 (over y, x).
Axes of the slice: x: 2, y: 2, z: 4, core: 2. Of those that a mesh axis runs over, the one named last changes fastest.
Arguments:
- loads: float32 [48, 1024, 4096], P(None, 'row', 'col'), may hold values from -6 to 6
- below_first: float32 [47, 1024, 1024], P(None, 'row', 'col'), may hold values from -0.1875 to 0.1875
- below_second: float32 [46, 1024, 1024], P(None, 'row', 'col'), may hold values from -0.1875 to 0.1875
- inverses: float32 [2, 1024, 1024], P(None, None, 'row'), may hold values from -1 to 2, as said below
Outputs:
- solved: float32 [2, 1024, 4096], P(None, None, 'col')
- remaining: float32 [46, 1024, 4096], P(None, 'row', 'col')
Inputs may be any that keep to these rules, and one draw needn't show every extreme that they name: `inverses`: each of the two matrices is lower triangular, with a diagonal from 0.5 to 2.
All inputs are finite; a program needn't handle non-finite values.
Results may differ from a plain program's by a relative error of at most 0.000084.
Values sent between devices are 32-bit elements; how exact they have to be, the bound alone decides.
A program may use at most 256 MiB of HBM per device.

v0:
```python
import functools
import jax
import jax.numpy as jnp
from jax import lax
from jax.experimental import pallas as pl
from jax.experimental.pallas import tpu as pltpu
from jax.sharding import PartitionSpec as P

HIGH = lax.Precision.HIGH
STEP = 4


def chunk_sizes(count):
    last = 4
    middle = count * 2 // 5 // 2 * 2
    return [count - middle - last, middle, last]


def halves(value):
    high = lax.reduce_precision(value, 8, 7)
    return high.astype(jnp.bfloat16), (value - high).astype(jnp.bfloat16)


def update_kernel(step, a1, a2, *refs):
    loads = refs[:step // 2]
    f1h, f1l, f2h, f2l = refs[step // 2:step // 2 + 4]
    out = refs[-1]
    rows = a1.shape[1]
    total = None
    for a, fh, fl in ((a1, f1h, f1l), (a2, f2h, f2l)):
        whole = a[...].reshape(step * rows, a.shape[2])
        high = whole.astype(jnp.bfloat16)
        low = (whole - high.astype(jnp.float32)).astype(jnp.bfloat16)
        for x, y in ((high, fh), (high, fl), (low, fh)):
            term = jnp.dot(x, y[...], preferred_element_type=jnp.float32)
            total = term if total is None else total + term
    total = total.reshape(step, rows, total.shape[1])
    for at, part in enumerate(loads):
        out[2 * at:2 * at + 2] = part[...] - total[2 * at:2 * at + 2]


def update_chunk(both, loads, factors, offset, previous):
    rows, depth = both.shape[1:]
    size = both.shape[0] // 2
    columns = loads.shape[2]
    count = loads.shape[0] - 2
    step = STEP if size % STEP == 0 and offset % STEP == 0 else 2
    pairs = step // 2
    block = pl.BlockSpec((step, rows, depth), lambda i: (i, 0, 0))
    block2 = pl.BlockSpec((step, rows, depth), lambda i: (size // step + i, 0, 0))
    load_specs = [
        pl.BlockSpec((2, rows, columns), lambda i, k=k: (1 + offset // 2 + i * pairs + k, 0, 0))
        for k in range(pairs)
    ]
    full = pl.BlockSpec((depth, columns), lambda i: (0, 0), pipeline_mode=pl.Buffered(1))
    operands = [both, both] + [loads] * pairs + list(factors)
    in_specs = [block, block2] + load_specs + [full] * 4
    aliases = {}
    if previous is not None:
        aliases = {len(operands): 0}
        operands.append(previous)
        in_specs.append(pl.BlockSpec(memory_space=pl.ANY))
    work = size * rows * depth * columns
    return pl.pallas_call(
        functools.partial(update_kernel, step),
        out_shape=jax.ShapeDtypeStruct((count, rows, columns), jnp.float32),
        grid=(size // step,),
        in_specs=in_specs,
        out_specs=pl.BlockSpec((step, rows, columns), lambda i: (offset // step + i, 0, 0)),
        input_output_aliases=aliases,
        compiler_params=pltpu.CompilerParams(vmem_limit_bytes=48 * 1024 * 1024),
        cost_estimate=pl.CostEstimate(
            flops=12 * work,
            bytes_accessed=8 * size * rows * (depth + columns) + 8 * depth * columns,
            transcendentals=0,
        ),
    )(*operands)


def local(loads, below_first, below_second, inverses):
    cycles = loads.shape[0]
    gather = lambda piece: lax.all_gather(piece, "col", axis=2, tiled=True)
    chunks, offsets = [], []
    at = 0
    for size in chunk_sizes(cycles - 2):
        chunks.append(jnp.concatenate([below_first[at + 1:at + 1 + size], below_second[at:at + size]]))
        offsets.append(at)
        at += size
    inverses, chunks[0] = lax.optimization_barrier((inverses, chunks[0]))
    early = gather(chunks[0])
    top = gather(below_first[:1])
    first_block = lax.psum(jnp.dot(inverses[0], loads[0], precision=HIGH), "row")
    first_block, later = lax.optimization_barrier((first_block, chunks[1:]))
    updated = loads[1] - jnp.dot(top[0], first_block, precision=HIGH)
    terms = jnp.dot(inverses[1], updated, precision=HIGH)
    terms, early = lax.optimization_barrier((terms, early))
    second_block = lax.psum(terms, "row")
    factors = halves(first_block) + halves(second_block)
    remaining = None
    for both, offset in zip([early] + [gather(chunk) for chunk in later], offsets):
        remaining = update_chunk(both, loads, factors, offset, remaining)
    return (jnp.stack([first_block, second_block]), remaining)


def solution(mesh):
    in_specs = (
        P(None, "row", "col"),
        P(None, "row", "col"),
        P(None, "row", "col"),
        P(None, None, "row"),
    )
    out_specs = (P(None, None, "col"), P(None, "row", "col"))
    return jax.shard_map(local, mesh=mesh, in_specs=in_specs, out_specs=out_specs, check_vma=False)
```

profile of v0, /device:TPU:16, one launch (start us, length us, event | category | flops | bytes accessed | tf_op | source)
XLA Modules:
  0.0 503.1 jit_solution(5230112477139280542)
XLA Ops:
  8.0 0.0 all-reduce.3.cloned.1.call-start
  8.0 0.0 slice-start
  8.1 0.0 slice-start.4
  8.1 1.9 slice-done
  9.9 1.0 slice-done.4
  10.9 3.2 pad_maximum_fusion.1
  14.1 5.0 fusion.6
  19.1 0.0 all-reduce.3.cloned.1.call-update
  19.1 0.0 all-gather.4.cloned.1.call-start
  19.1 0.5 all-gather.4.cloned.1.call-update
  19.7 0.0 all-reduce.5.cloned.1.call-start
  19.7 0.0 slice-start.3
  19.7 0.0 slice-start.2
  19.7 0.0 slice-start.5
  19.8 0.0 slice-start.1
  19.8 3.5 slice.38
  23.3 0.0 slice-done.3
  23.3 10.0 %all_gather.12 = f32[1,128,1024]{2,1,0:T(8,128)S(1)} all-gather(f32[1,128,256]{2,1,0:T(8,128)S(1)} %slice-done.3), channel_id=1, replica_groups=mesh['row'=8,'col'=4] {'col'}, dimensions={2}, use_global_device_ids=true | all-gather | bytes 655360 | tf_op jit(solution)/shard_map/all_gather | solution.py:82
  33.3 0.0 slice-done.2
  33.3 0.0 slice-done.5
  33.3 1.1 pad_maximum_fusion.3
  34.4 0.0 slice-done.1
  34.4 5.2 %pad_maximum_fusion.2 = f32[36,128,256]{2,1,0:T(8,128)} fusion(f32[18,128,256]{2,1,0:T(8,128)} %slice.38, f32[18,128,256]{2,1,0:T(8,128)S(1)} %slice-done.1), kind=kLoop, calls=%fused_computation.6 | loop fusion | flops 1179648 | bytes 9437184 | tf_op jit(solution)/shard_map/concatenate | solution.py:86
  39.6 0.0 copy-start.4
  39.6 77.2 %all-reduce.3.cloned.1.call-done = f32[1024,1024]{1,0:T(8,128)} async-done(((f32[1024,1024]{1,0:T(8,128)}), f32[1024,1024]{1,0:T(8,128)}) %all-reduce.3.cloned.1.call-update) | async-done | bytes 4194320 | tf_op jit(solution)/shard_map/psum | solution.py:92
  116.8 3.7 fusion.2
  120.5 0.0 copy-done.4
  120.5 3.8 fusion.4
  124.3 126.2 %all-gather.4.cloned.1.call-done.a1.a2 = f32[48,128,1024]{2,1,0:T(8,128)} async-done(((f32[48,128,256]{2,1,0:T(8,128)}), f32[48,128,1024]{2,1,0:T(8,128)}) %all-gather.4.cloned.1.call-update) | async-done | bytes 25165840 | tf_op jit(solution)/shard_map/all_gather | solution.py:82
  250.5 0.0 all-reduce.5.cloned.1.call-update
  250.5 0.0 all-gather.8.cloned.1.call-start
  250.6 0.5 all-gather.8.cloned.1.call-update
  251.1 0.0 all-gather.6.cloned.1.call-start
  251.2 4.5 fusion
  255.7 0.0 all-gather.6.cloned.1.call-update
  255.7 91.5 %all-reduce.5.cloned.1.call-done = f32[1024,1024]{1,0:T(8,128)} async-done(((f32[1024,1024]{1,0:T(8,128)}), f32[1024,1024]{1,0:T(8,128)}) %all-reduce.5.cloned.1.call-update) | async-done | bytes 4194320 | tf_op jit(solution)/shard_map/psum | solution.py:97
  347.2 0.0 copy-start.3
  347.2 9.0 %pad_maximum_fusion = f32[2,1024,1024]{2,1,0:T(8,128)} fusion(f32[1,1024,1024]{2,1,0:T(8,128)} %bitcast.23, f32[1,1024,1024]{2,1,0:T(8,128)} %bitcast.22), kind=kLoop, calls=%fused_computation | loop fusion | flops 2097152 | bytes 16777216 | tf_op jit(solution)/shard_map/stack | solution.py:102
  356.2 0.0 copy-done.3
  356.2 0.0 copy-start
  356.2 2.9 fusion.1
  359.1 0.0 copy-done
  359.1 46.4 %shard_map.59.refs_5_ = f32[46,128,1024]{2,1,0:T(8,128)} custom-call(f32[48,128,1024]{2,1,0:T(8,128)} %all-gather.4.cloned.1.call-done.a1.a2, f32[48,128,1024]{2,1,0:T(8,128)} %all-gather.4.cloned.1.call-done.a1.a2, f32[48,128,1024]{2,1,0:T(8,128)} %refs_0_.5, f32[48,128,1024]{2,1,0:T(8,128)} %refs_0_.5, bf16[1024,1024]{1,0:T(8,128)(2,1)S(1)} %copy-done, ...), custom_call_target="tpu_custom_call" | custom-call | flops 38654705664 | bytes 58720256 | tf_op jit(solution)/shard_map/pallas_call | solution.py:64
  405.5 23.0 %all-gather.8.cloned.1.call-done.a1.a2 = f32[36,128,1024]{2,1,0:T(8,128)} async-done(((f32[36,128,256]{2,1,0:T(8,128)}), f32[36,128,1024]{2,1,0:T(8,128)}) %all-gather.8.cloned.1.call-update) | async-done | bytes 18874384 | tf_op jit(solution)/shard_map/all_gather | solution.py:82
  428.5 0.0 copy-start.1
  428.5 1.6 copy-done.1
  430.1 35.5 %shard_map.60.refs_5_ = f32[46,128,1024]{2,1,0:T(8,128)} custom-call(f32[36,128,1024]{2,1,0:T(8,128)} %all-gather.8.cloned.1.call-done.a1.a2, f32[36,128,1024]{2,1,0:T(8,128)} %all-gather.8.cloned.1.call-done.a1.a2, f32[48,128,1024]{2,1,0:T(8,128)} %refs_0_.5, bf16[1024,1024]{1,0:T(8,128)(2,1)S(1)} %copy-done.1, ...), custom_call_target="tpu_custom_call", output_to_operand_aliasing={{}: (7, {})} | custom-call | flops 28991029248 | bytes 46137344 | tf_op jit(solution)/shard_map/pallas_call | solution.py:64
  465.6 17.0 %all-gather.6.cloned.1.call-done.a1.a2 = f32[8,128,1024]{2,1,0:T(8,128)} async-done(((f32[8,128,256]{2,1,0:T(8,128)}), f32[8,128,1024]{2,1,0:T(8,128)}) %all-gather.6.cloned.1.call-update) | async-done | bytes 4194320 | tf_op jit(solution)/shard_map/all_gather | solution.py:82
  482.6 0.0 copy-start.2
  482.6 1.6 copy-done.2
  484.2 11.3 %shard_map.61 = f32[46,128,1024]{2,1,0:T(8,128)} custom-call(f32[8,128,1024]{2,1,0:T(8,128)} %all-gather.6.cloned.1.call-done.a1.a2, f32[8,128,1024]{2,1,0:T(8,128)} %all-gather.6.cloned.1.call-done.a1.a2, f32[48,128,1024]{2,1,0:T(8,128)} %refs_0_.5, bf16[1024,1024]{1,0:T(8,128)(2,1)S(1)} %copy-done.2, ...), custom_call_target="tpu_custom_call", output_to_operand_aliasing={{}: (7, {})} | custom-call | flops 6442450944 | bytes 16777216 | tf_op jit(solution)/shard_map/pallas_call | solution.py:64
Async XLA Ops:
  8.0 108.8 %all-reduce.3.cloned.1.call-start = ((), (), s32[]{:S(2)}) async-start(), calls=%async_computation | async-start | bytes 8388608 | tf_op jit(solution)/shard_map/psum | solution.py:92
  8.0 1.9 slice-start
  8.1 2.8 slice-start.4
  19.1 231.4 %all-gather.4.cloned.1.call-start = ((), (), s32[]{:S(2)}) async-start(), calls=%async_computation.1 | async-start | bytes 31457280 | tf_op jit(solution)/shard_map/all_gather | solution.py:82
  19.7 327.5 %all-reduce.5.cloned.1.call-start = ((), (), s32[]{:S(2)}) async-start(), calls=%async_computation.2 | async-start | bytes 8388608 | tf_op jit(solution)/shard_map/psum | solution.py:97
  19.7 3.6 slice-start.3
  19.7 13.6 %slice-start.2 = ((f32[47,128,256]{2,1,0:T(8,128)}), f32[4,128,256]{2,1,0:T(8,128)S(1)}, s32[]{:S(2)}) async-start(f32[47,128,256]{2,1,0:T(8,128)} %param.5), calls=%async_computation.7 | async-start | bytes 1048576 | tf_op jit(solution)/shard_map/slice | solution.py:86
  19.7 13.6 %slice-start.5 = ((f32[46,128,256]{2,1,0:T(8,128)}), f32[4,128,256]{2,1,0:T(8,128)S(1)}, s32[]{:S(2)}) async-start(f32[46,128,256]{2,1,0:T(8,128)} %param.6), calls=%async_computation.10 | async-start | bytes 1048576 | tf_op jit(solution)/shard_map/slice | solution.py:86
  19.8 14.7 %slice-start.1 = ((f32[47,128,256]{2,1,0:T(8,128)}), f32[18,128,256]{2,1,0:T(8,128)S(1)}, s32[]{:S(2)}) async-start(f32[47,128,256]{2,1,0:T(8,128)} %param.5), calls=%async_computation.6 | async-start | bytes 4718592 | tf_op jit(solution)/shard_map/slice | solution.py:86
  39.6 80.9 %copy-start.4 = (f32[2,1024,128]{2,1,0:T(8,128)S(1)}, f32[2,1024,128]{2,1,0:T(8,128)}, u32[]{:S(2)}) copy-start(f32[2,1024,128]{2,1,0:T(8,128)} %param.7) | copy-start | bytes 3145732
  250.5 178.0 %all-gather.8.cloned.1.call-start = ((), (), s32[]{:S(2)}) async-start(), calls=%async_computation.4 | async-start | bytes 23592960 | tf_op jit(solution)/shard_map/all_gather | solution.py:82
  251.1 231.5 %all-gather.6.cloned.1.call-start = ((), (), s32[]{:S(2)}) async-start(), calls=%async_computation.3 | async-start | bytes 5242880 | tf_op jit(solution)/shard_map/all_gather | solution.py:82
  347.2 9.0 %copy-start.3 = (f32[1024,1024]{1,0:T(8,128)S(1)}, f32[1024,1024]{1,0:T(8,128)}, u32[]{:S(2)}) copy-start(f32[1024,1024]{1,0:T(8,128)} %all-reduce.5.cloned.1.call-done) | copy-start | bytes 12582916
  356.2 2.9 copy-start
  428.5 1.6 copy-start.1
  482.6 1.6 copy-start.2
Sparse Core Ops, SparseCore 0:
  19.2 97.5 all-reduce.2
  250.6 96.4 all-reduce.4
Sparse Core Ops, SparseCore 1:
  22.0 228.4 all-gather.3
  252.8 175.6 all-gather.7
  430.2 52.4 all-gather.5
where the time goes:
time: 505 us; the launch traced here: 503 us
  waiting for transfers between devices  336 us (67%)
  Pallas kernels  93.2 us (18%)
  other arithmetic  25.9 us (5%)
  between operations  15.7 us (3%)
  matrix products  12.5 us (2%)
  blocking collectives  10 us (2%)
  local copies, waits for them, and re-layouts  9.55 us (2%)
    all_gather x3, waiting for transfers between devices, local(): gather = lambda piece: lax.all_gather(piece, 'col', axis=2, tiled=True)  166 us
    pallas_call x3, Pallas kernels, update_chunk(): pl.pallas_call(functools.partial(update_kernel, step), out_shape=jax.Shap...  93.2 us
    psum x1, waiting for transfers between devices, local(): second_block = lax.psum(terms, 'row')  91.5 us
    psum x1, waiting for transfers between devices, local(): lax.psum(jnp.dot(inverses[0], loads[0], precision=HIGH), 'row')  77.2 us
  transfers between devices with their start and end apart: 5, of which 5 were waited for; matrix products, arithmetic and copies ran while one was open for 7% of the time, Pallas kernels for 16%

commit v1 on v0

v1 whole, which is shorter than its diff:
```python
import functools
import jax
import jax.numpy as jnp
from jax import lax
from jax.experimental import pallas as pl
from jax.experimental.pallas import tpu as pltpu
from jax.sharding import PartitionSpec as P

HIGH = lax.Precision.HIGH
MESH = pl.DeviceIdType.MESH
STEPS = 4


def chunk_sizes(count):
    sizes = []
    for size in (8, 4, 2):
        while count - size >= size // 2:
            sizes.append(size)
            count -= size
    return sizes + [count] if count else sizes


def halves(value):
    high = value.astype(jnp.bfloat16)
    return high, (value - high.astype(jnp.float32)).astype(jnp.bfloat16)


def product(x, y):
    dot = functools.partial(jnp.dot, preferred_element_type=jnp.float32)
    return dot(x[0], y[0]) + dot(x[0], y[1]) + dot(x[1], y[0])


def solve_kernel(sizes, loads, first, second, inverses, *refs):
    count = len(sizes)
    solved, (high, low, x1, y2, d1, d2) = refs[:2], refs[2:8]
    x2, y1 = refs[8:8 + count], refs[8 + count:8 + 2 * count]
    (inv, rhs, top, part, swapped, passed, block, high_stage, low_stage,
     local_sem, link_send, link_recv, sum_send, sum_recv) = refs[8 + 2 * count:]
    r, c = lax.axis_index("row"), lax.axis_index("col")
    z, core = r // 2, lax.rem(r, 2)
    chips = inv.shape[1] // inv.shape[2] // 2
    rows = inv.shape[2]
    width = first.shape[2]
    x_side = c + 1 - 2 * lax.rem(c, 2)
    y_side = lax.rem(c + 2, 4)
    x_to, y_to = (r, x_side), (r, y_side)
    core_to = (r + 1 - 2 * core, c)

    def z_place(d):
        return lax.rem(z + d + chips, chips)

    def z_to(d):
        return (z_place(d) * 2 + core, c)

    def remote(src, dst, sends, recvs, at, to):
        return pltpu.make_async_remote_copy(src, dst, sends.at[at], recvs.at[at], device_id=to, device_id_type=MESH)

    inv_in = pltpu.make_async_copy(inverses, inv, local_sem.at[0])
    rhs_in = pltpu.make_async_copy(loads.at[pl.ds(0, 2)], rhs, local_sem.at[1])
    top_in = pltpu.make_async_copy(first.at[0], top.at[c], local_sem.at[2])
    inv_in.start()
    rhs_in.start()
    top_in.start()

    barrier = pltpu.get_barrier_semaphore()
    partners = [x_to, y_to, core_to] + [z_to(d) for d in range(1, chips)]
    for to in partners:
        pl.semaphore_signal(barrier, inc=1, device_id=to, device_id_type=MESH)
    pl.semaphore_wait(barrier, len(partners))

    top_in.wait()
    link = functools.partial(remote, sends=link_send, recvs=link_recv)
    top_x = link(top.at[c], top.at[c], at=0, to=x_to)
    top_y = link(top.at[c], top.at[c], at=1, to=y_to)
    top_d = link(top.at[y_side], top.at[y_side], at=2, to=x_to)
    total_blocks = sum(sizes)
    send_x1 = link(first.at[pl.ds(1, total_blocks)], x1, at=3, to=x_to)
    send_y2 = link(second, y2, at=4, to=y_to)
    send_d1 = link(y1[0], d1, at=5, to=x_to)
    send_d2 = link(x2[0], d2, at=6, to=y_to)
    send_x2, send_y1 = [], []
    start = 0
    for k, size in enumerate(sizes):
        send_x2.append(link(second.at[pl.ds(start, size)], x2[k], at=7 + k, to=x_to))
        send_y1.append(link(first.at[pl.ds(start + 1, size)], y1[k], at=7 + count + k, to=y_to))
        start += size
    for copy in (top_x, top_y, send_x2[0], send_y1[0]):
        copy.start()

    def top_recv(q, at):
        link(top.at[q], top.at[q], at=at, to=x_to).wait_recv()

    def finish(j, before, between):
        base = j * (4 * chips)
        at = functools.partial(remote, sends=sum_send, recvs=sum_recv)
        away = at(part.at[j, pl.ds((1 - core) * chips, chips)], swapped.at[j], at=base, to=core_to)
        away.start()
        before()
        away.wait_recv()

        @pl.loop(0, chips)
        def _(i):
            part[j, core * chips + i] += swapped[j, i]

        out = []
        for d in range(1, chips):
            copy = at(part.at[j, core * chips + z_place(d)], passed.at[j, d - 1], at=base + d, to=z_to(d))
            copy.start()
            out.append(copy)
        between()
        for copy in out:
            copy.wait_recv()
        mine = pl.ds(pl.multiple_of(r * rows, rows), rows)
        total = part[j, core * chips + z]
        for d in range(1, chips):
            total = total + passed[j, d - 1]
        block[j, mine] = total
        gathered = []
        for d in range(1, chips):
            copy = at(block.at[j, mine], block.at[j, mine], at=base + chips - 1 + d, to=z_to(d))
            copy.start()
            gathered.append(copy)
        across = [at(block.at[j, mine], block.at[j, mine], at=base + 2 * chips - 1, to=core_to)]
        across[0].start()
        return away, out, gathered, across, base, at

    def complete(j, state):
        away, out, gathered, across, base, at = state
        for d in range(1, chips):
            here = pl.ds(pl.multiple_of((z_place(-d) * 2 + core) * rows, rows), rows)
            at(block.at[j, here], block.at[j, here], at=base + chips - 1 + d, to=z_to(d)).wait_recv()
            copy = at(block.at[j, here], block.at[j, here], at=base + 2 * chips - 1 + d, to=core_to)
            copy.start()
            across.append(copy)
        for d in range(chips):
            there = pl.ds(pl.multiple_of((z_place(-d) * 2 + 1 - core) * rows, rows), rows)
            at(block.at[j, there], block.at[j, there], at=base + 2 * chips - 1 + d, to=core_to).wait_recv()
        for copy in [away] + out + gathered + across:
            copy.wait_send()

    def term(j, right):
        @pl.loop(0, 2 * chips)
        def _(i):
            owner = lax.rem(i, chips) * 2 + i // chips
            left = inv[j, pl.ds(pl.multiple_of(owner * rows, rows), rows)]
            part[j, i] = product(halves(left), right)

    def stage(j):
        for k, q in enumerate((c, x_side, y_side, 3 - c)):
            quarter = block[j, pl.ds(pl.multiple_of(q * width, width), width)]
            h, l = halves(quarter)
            high_stage[j, k * width:(k + 1) * width] = h
            low_stage[j, k * width:(k + 1) * width] = l
        depth = 4 * width
        copies = [
            pltpu.make_async_copy(block.at[j], solved[j], local_sem.at[3 + 3 * j]),
            pltpu.make_async_copy(high_stage.at[j], high.at[pl.ds(j * depth, depth)], local_sem.at[4 + 3 * j]),
            pltpu.make_async_copy(low_stage.at[j], low.at[pl.ds(j * depth, depth)], local_sem.at[5 + 3 * j]),
        ]
        for copy in copies:
            copy.start()
        return copies

    inv_in.wait()
    rhs_in.wait()
    term(0, halves(rhs[0]))

    def forward_top():
        top_recv(y_side, 1)
        top_d.start()
        for copy in send_x2[1:] + send_y1[1:]:
            copy.start()

    def queue_rest():
        send_x1.start()
        send_y2.start()

    def forward_first():
        send_y1[0].wait_recv()
        send_d1.start()
        send_x2[0].wait_recv()
        send_d2.start()

    def nothing():
        pass

    state = finish(0, forward_top, queue_rest)
    complete(0, state)
    copies = stage(0)
    top_recv(x_side, 0)
    top_recv(3 - c, 2)
    update = rhs[1]
    for q in range(4):
        left = halves(top[q])
        right = halves(block[0, q * width:(q + 1) * width])
        update = update - product(left, right)
    term(1, halves(update))

    state = finish(1, nothing, forward_first)
    complete(1, state)
    copies += stage(1)
    for copy in copies:
        copy.wait()
    for copy in (top_x, top_y, top_d):
        copy.wait_send()
    for copy in [send_x1, send_y2, send_d1, send_d2] + send_x2[1:] + send_y1[1:]:
        copy.wait()
    for copy in (send_x2[0], send_y1[0]):
        copy.wait_send()


def solve(sizes, row_count, loads, first, second, inverses):
    chips = row_count // 2
    rows, columns = loads.shape[1:]
    width = first.shape[2]
    depth = 4 * width
    f32, bf16 = jnp.float32, jnp.bfloat16
    anywhere = pl.BlockSpec(memory_space=pl.ANY)
    shape = jax.ShapeDtypeStruct
    piece = lambda size: shape((size, rows, width), f32)
    pieces = [piece(size) for size in [sum(sizes)] * 2 + [sizes[0]] * 2 + list(sizes) * 2]
    links = 7 + 2 * len(sizes)
    sums = 2 * 4 * chips
    return pl.pallas_call(
        functools.partial(solve_kernel, sizes),
        out_shape=[shape((depth, columns), f32)] * 2 + [shape((2 * depth, columns), bf16)] * 2 + pieces,
        in_specs=[anywhere] * 4,
        out_specs=[anywhere] * (4 + len(pieces)),
        scratch_shapes=[
            pltpu.VMEM((2, depth, rows), f32),
            pltpu.VMEM((2, rows, columns), f32),
            pltpu.VMEM((4, rows, width), f32),
            pltpu.VMEM((2, 2 * chips, rows, columns), f32),
            pltpu.VMEM((2, chips, rows, columns), f32),
            pltpu.VMEM((2, chips - 1, rows, columns), f32),
            pltpu.VMEM((2, depth, columns), f32),
            pltpu.VMEM((2, depth, columns), bf16),
            pltpu.VMEM((2, depth, columns), bf16),
            pltpu.SemaphoreType.DMA((9,)),
            pltpu.SemaphoreType.DMA((links,)),
            pltpu.SemaphoreType.DMA((links,)),
            pltpu.SemaphoreType.DMA((sums,)),
            pltpu.SemaphoreType.DMA((sums,)),
        ],
        compiler_params=pltpu.CompilerParams(
            collective_id=0, has_side_effects=True, vmem_limit_bytes=60 * 1024 * 1024,
        ),
    )(loads, first, second, inverses)


def update_kernel(count, step, *refs):
    pieces = refs[:count]
    loads = refs[count:count + step // 2]
    high_ref, low_ref = refs[count + step // 2:count + step // 2 + 2]
    out, ah, al = refs[-3:]
    rows, width = pieces[0].shape[1:]
    for at, piece in enumerate(pieces):
        high, low = halves(piece[...].reshape(step * rows, width))
        ah[:, at * width:(at + 1) * width] = high
        al[:, at * width:(at + 1) * width] = low
    total = product((ah[...], al[...]), (high_ref[...], low_ref[...]))
    total = total.reshape(step, rows, total.shape[1])
    for at, part in enumerate(loads):
        out[2 * at:2 * at + 2] = part[...] - total[2 * at:2 * at + 2]


def update_chunk(firsts, seconds, loads, high, low, offset, size, previous):
    rows, width = firsts[0][0].shape[1:]
    columns = loads.shape[2]
    depth = high.shape[0]
    count = loads.shape[0] - 2
    step = STEPS if size % STEPS == 0 and offset % STEPS == 0 else 2
    operands, in_specs = [], []
    for array, at in firsts + seconds:
        operands.append(array)
        in_specs.append(pl.BlockSpec(
            (pl.Element(step), pl.Element(rows), pl.Element(width)),
            lambda i, at=at: (at + i * step, 0, 0)))
    for k in range(step // 2):
        operands.append(loads)
        in_specs.append(pl.BlockSpec((2, rows, columns), lambda i, k=k: (1 + (offset + i * step) // 2 + k, 0, 0)))
    for factor in (high, low):
        operands.append(factor)
        in_specs.append(pl.BlockSpec((depth, columns), lambda i: (0, 0), pipeline_mode=pl.Buffered(1)))
    aliases = {}
    if previous is not None:
        aliases = {len(operands): 0}
        operands.append(previous)
        in_specs.append(pl.BlockSpec(memory_space=pl.ANY))
    work = size * rows * depth * columns
    return pl.pallas_call(
        functools.partial(update_kernel, len(firsts + seconds), step),
        out_shape=jax.ShapeDtypeStruct((count, rows, columns), jnp.float32),
        grid=(size // step,),
        in_specs=in_specs,
        out_specs=pl.BlockSpec((step, rows, columns), lambda i: (offset // step + i, 0, 0)),
        scratch_shapes=[pltpu.VMEM((step * rows, depth), jnp.bfloat16)] * 2,
        input_output_aliases=aliases,
        compiler_params=pltpu.CompilerParams(vmem_limit_bytes=60 * 1024 * 1024),
        cost_estimate=pl.CostEstimate(
            flops=6 * work,
            bytes_accessed=4 * size * rows * (depth + 2 * columns) + 4 * depth * columns,
            transcendentals=0,
        ),
    )(*operands)


def local_quarters(row_count, loads, below_first, below_second, inverses):
    sizes = chunk_sizes(loads.shape[0] - 2)
    along_x = [(c, c ^ 1) for c in range(4)]
    along_y = [(c, c ^ 2) for c in range(4)]
    results = solve(sizes, row_count, loads, below_first, below_second, inverses)
    solved, (high, low, x1, y2, d1, d2) = results[:2], results[2:8]
    x2, y1 = results[8:8 + len(sizes)], results[8 + len(sizes):]
    solved, high = lax.optimization_barrier((jnp.stack(solved), high))
    d1 = [d1] + [lax.ppermute(piece, "col", along_x) for piece in y1[1:]]
    d2 = [d2] + [lax.ppermute(piece, "col", along_y) for piece in x2[1:]]
    remaining = None
    at = 0
    for k, size in enumerate(sizes):
        firsts = [(below_first, at + 1), (x1, at), (y1[k], 0), (d1[k], 0)]
        seconds = [(below_second, at), (x2[k], 0), (y2, at), (d2[k], 0)]
        remaining = update_chunk(firsts, seconds, loads, high, low, at, size, remaining)
        at += size
    return solved, remaining


def local_gathered(loads, below_first, below_second, inverses):
    count = loads.shape[0] - 2
    gather = lambda piece: lax.all_gather(piece, "col", axis=2, tiled=True)
    top = gather(below_first[:1])
    first_block = lax.psum(jnp.dot(inverses[0], loads[0], precision=HIGH), "row")
    updated = loads[1] - jnp.dot(top[0], first_block, precision=HIGH)
    second_block = lax.psum(jnp.dot(inverses[1], updated, precision=HIGH), "row")
    solved = jnp.stack([first_block, second_block])
    whole = solved.reshape(-1, solved.shape[2])
    high = lax.reduce_precision(whole, 8, 7)
    high, low = high.astype(jnp.bfloat16), (whole - high).astype(jnp.bfloat16)
    remaining = None
    at = 0
    for size in (count // 8 * 4, count - count // 8 * 4):
        firsts = [(gather(below_first[at + 1:at + 1 + size]), 0)]
        seconds = [(gather(below_second[at:at + size]), 0)]
        remaining = update_chunk(firsts, seconds, loads, high, low, at, size, remaining)
        at += size
    return solved, remaining


def solution(mesh):
    in_specs = (
        P(None, "row", "col"),
        P(None, "row", "col"),
        P(None, "row", "col"),
        P(None, None, "row"),
    )
    out_specs = (P(None, None, "col"), P(None, "row", "col"))
    quarters = mesh.shape["col"] == 4 and mesh.shape["row"] % 2 == 0
    local = functools.partial(local_quarters, mesh.shape["row"]) if quarters else local_gathered
    return jax.shard_map(local, mesh=mesh, in_specs=in_specs, out_specs=out_specs, check_vma=False)
```

time: 505 us -> 444 us (0.88)
  waiting for transfers between devices: 336 us -> 0.03 us
  Pallas kernels: 93.2 us -> 417 us
  other arithmetic: 25.9 us -> 8.53 us
  between operations: 15.7 us -> 0.75 us
  starting transfers between devices: 0.2 us -> 12.9 us
  matrix products: 12.5 us -> 0 us
  blocking collectives: 10 us -> 0 us
  local copies, waits for them, and re-layouts: 9.55 us -> 1.4 us
    pallas_call x3 -> x8, Pallas kernels: 93.2 us -> 417 us  [the longest x1 291 us: solve(): pl.pallas_call(functools.partial(solve_kernel, sizes), out_shape=[shape((...]
    psum x2 -> x0, waiting for transfers between devices: 169 us -> none  [the longest x1 91.5 us: local(): second_block = lax.psum(terms, 'row')]
    all_gather x3 -> x0, waiting for transfers between devices: 166 us -> none  [local(): gather = lambda piece: lax.all_gather(piece, 'col', axis=2, tiled=True)]
    ppermute x0 -> x12, starting transfers between devices: none -> 12.9 us  [the longest x6 6.68 us: local_quarters(): d2 = [d2] + [lax.ppermute(piece, 'col', along_y) for piece in x2[1:]]]
    dot_general x3 -> x0, matrix products: 12.5 us -> none  [the longest x1 4.99 us: local(): jnp.dot(inverses[0], loads[0], precision=HIGH)]
    all_gather x1 -> x0, blocking collectives: 10 us -> none  [local(): gather = lambda piece: lax.all_gather(piece, 'col', axis=2, tiled=True)]
    concatenate x3 -> x0, other arithmetic: 9.45 us -> none  [local(): jnp.concatenate([below_first[at + 1:at + 1 + size], below_second[at:at +...]
    convert_element_type x2 -> x0, other arithmetic: 7.44 us -> none  [halves(): return (high.astype(jnp.bfloat16), (value - high).astype(jnp.bfloat16))]
  transfers between devices with their start and end apart: 5 -> 12, of which waited for: 5 -> 0; matrix products, arithmetic and copies ran while one was open for 7% -> 2% of each run, Pallas kernels for 16% -> 27%
where the time goes in v1:
time: 444 us; the launch traced here: 441 us
  Pallas kernels  417 us (94%)
  starting transfers between devices  12.9 us (3%)
  other arithmetic  8.53 us (2%)
    pallas_call x1, Pallas kernels, solve(): pl.pallas_call(functools.partial(solve_kernel, sizes), out_shape=[shape((...  291 us
    pallas_call x7, Pallas kernels, update_chunk(): pl.pallas_call(functools.partial(update_kernel, len(firsts + seconds), st...  126 us
  transfers between devices with their start and end apart: 12, of which 0 were waited for; matrix products, arithmetic and copies ran while one was open for 2% of the time, Pallas kernels for 27%

profile of v1, /device:TPU:16, one launch (start us, length us, event | category | flops | bytes accessed | tf_op | source)
XLA Modules:
  0.0 440.8 jit_solution(2038845235299822085)
XLA Ops:
  0.6 291.4 %shard_map.59 = (f32[1024,1024]{1,0:T(8,128)}, f32[1024,1024]{1,0:T(8,128)}, bf16[2048,1024]{1,0:T(8,128)(2,1)}, bf16[2048,1024]{1,0:T(8,128)(2,1)}, f32[46,128,...) custom-call(f32[48,128,1024]{2,1,0:T(8,128)} %refs_8_.13, ...), custom_call_target="tpu_custom_call" | custom-call | tf_op jit(solution)/shard_map/pallas_call | solution.py:224
  292.0 0.6 collective-permute-start.10
  292.6 1.5 collective-permute-start.11
  294.2 1.5 collective-permute-start.8
  295.7 0.5 collective-permute-start.9
  296.2 0.5 collective-permute-start.6
  296.7 8.5 %pad_maximum_fusion = f32[2,1024,1024]{2,1,0:T(8,128)} fusion(f32[1,1024,1024]{2,1,0:T(8,128)} %bitcast.3, f32[1,1024,1024]{2,1,0:T(8,128)} %bitcast.2), kind=kLoop, calls=%fused_computation | loop fusion | flops 2097152 | bytes 16777216 | tf_op jit(solution)/shard_map/stack | solution.py:315
  305.2 0.0 copy-start.2
  305.2 0.0 copy-start.1
  305.2 20.7 %shard_map.60.refs_12_ = f32[46,128,1024]{2,1,0:T(8,128)} custom-call(f32[47,128,256]{2,1,0:T(8,128)} %refs_0_.13, f32[46,128,256]{2,1,0:T(8,128)} %get-tuple-element.30.refs_1_, f32[8,128,256]{2,1,0:T(8,128)} %get-tuple-element.46.refs_2_, f32[8,128,256]{2,1,0:T(8,128)} %get-tuple-element.47.refs_3_, f32[46,128,256]{2,1,0:T(8,128)} %refs_4_.13, ...), custom_call_target="tpu_custom_call" | custom-call | flops 12884901888 | bytes 25165824 | tf_op jit(solution)/shard_map/pallas_call | solution.py:291
  326.0 0.0 collective-permute-done.10.refs_3_
  326.0 0.0 copy-start.3
  326.0 0.0 copy-done.2
  326.0 1.6 collective-permute-start.7
  327.6 0.0 collective-permute-done.11.refs_7_
  327.6 0.0 copy-done.3
  327.6 0.0 copy-done.1
  327.6 0.0 copy-start
  327.6 1.6 collective-permute-start.4
  329.2 20.8 %shard_map.61.refs_12_ = f32[46,128,1024]{2,1,0:T(8,128)} custom-call(f32[47,128,256]{2,1,0:T(8,128)} %refs_0_.13, f32[46,128,256]{2,1,0:T(8,128)} %get-tuple-element.30.refs_1_, f32[8,128,256]{2,1,0:T(8,128)} %get-tuple-element.44.refs_2_, f32[8,128,256]{2,1,0:T(8,128)} %copy-done.3, f32[46,128,256]{2,1,0:T(8,128)} %refs_4_.13, ...), custom_call_target="tpu_custom_call", output_to_operand_aliasing={{}: (12, {})} | custom-call | flops 12884901888 | bytes 25165824 | tf_op jit(solution)/shard_map/pallas_call | solution.py:291
  350.0 0.0 collective-permute-done.8.refs_3_
  350.0 0.0 copy-done
  350.0 0.9 collective-permute-start.5
  350.9 0.0 collective-permute-done.9.refs_7_
  350.9 0.0 copy-start.4
  350.9 0.0 copy-start.6
  350.9 0.5 collective-permute-start.2
  351.5 20.7 %shard_map.62.refs_12_ = f32[46,128,1024]{2,1,0:T(8,128)} custom-call(f32[47,128,256]{2,1,0:T(8,128)} %refs_0_.13, f32[46,128,256]{2,1,0:T(8,128)} %get-tuple-element.30.refs_1_, f32[8,128,256]{2,1,0:T(8,128)} %get-tuple-element.42.refs_2_, f32[8,128,256]{2,1,0:T(8,128)} %collective-permute-done.8.refs_3_, ...), custom_call_target="tpu_custom_call", output_to_operand_aliasing={{}: (12, {})} | custom-call | flops 12884901888 | bytes 25165824 | tf_op jit(solution)/shard_map/pallas_call | solution.py:291
  372.1 0.0 collective-permute-done.6.refs_3_
  372.1 0.0 copy-done.4
  372.1 1.2 collective-permute-start.3
  373.4 0.0 collective-permute-done.7.refs_7_
  373.4 0.0 copy-done.6
  373.4 0.0 copy-start.5
  373.4 1.6 collective-permute-start
  374.9 20.9 %shard_map.63.refs_12_ = f32[46,128,1024]{2,1,0:T(8,128)} custom-call(f32[47,128,256]{2,1,0:T(8,128)} %refs_0_.13, f32[46,128,256]{2,1,0:T(8,128)} %get-tuple-element.30.refs_1_, f32[8,128,256]{2,1,0:T(8,128)} %get-tuple-element.40.refs_2_, f32[8,128,256]{2,1,0:T(8,128)} %collective-permute-done.6.refs_3_, ...), custom_call_target="tpu_custom_call", output_to_operand_aliasing={{}: (12, {})} | custom-call | flops 12884901888 | bytes 25165824 | tf_op jit(solution)/shard_map/pallas_call | solution.py:291
  395.8 0.0 collective-permute-done.4.refs_3_
  395.8 0.0 copy-done.5
  395.8 0.9 collective-permute-start.1
  396.7 0.0 collective-permute-done.5.refs_7_
  396.7 20.7 %shard_map.64.refs_12_ = f32[46,128,1024]{2,1,0:T(8,128)} custom-call(f32[47,128,256]{2,1,0:T(8,128)} %refs_0_.13, f32[46,128,256]{2,1,0:T(8,128)} %get-tuple-element.30.refs_1_, f32[8,128,256]{2,1,0:T(8,128)} %get-tuple-element.38.refs_2_, f32[8,128,256]{2,1,0:T(8,128)} %collective-permute-done.4.refs_3_, ...), custom_call_target="tpu_custom_call", output_to_operand_aliasing={{}: (12, {})} | custom-call | flops 12884901888 | bytes 25165824 | tf_op jit(solution)/shard_map/pallas_call | solution.py:291
  417.4 0.0 collective-permute-done.2.refs_3_
  417.4 0.0 collective-permute-done.3.refs_7_
  417.4 13.3 %shard_map.65.refs_11_ = f32[46,128,1024]{2,1,0:T(8,128)} custom-call(f32[47,128,256]{2,1,0:T(8,128)} %refs_0_.13, f32[46,128,256]{2,1,0:T(8,128)} %get-tuple-element.30.refs_1_, f32[4,128,256]{2,1,0:T(8,128)} %get-tuple-element.36.refs_2_, f32[4,128,256]{2,1,0:T(8,128)} %collective-permute-done.2.refs_3_, ...), custom_call_target="tpu_custom_call", output_to_operand_aliasing={{}: (12, {})} | custom-call | flops 6442450944 | bytes 16777216 | tf_op jit(solution)/shard_map/pallas_call | solution.py:291
  430.7 0.0 collective-permute-done.refs_3_
  430.7 0.0 copy-start.7
  430.7 0.0 collective-permute-done.1.refs_7_
  430.7 0.7 copy-done.7
  431.4 0.0 copy-start.8
  431.4 0.7 copy-done.8
  432.1 8.8 %shard_map.66 = f32[46,128,1024]{2,1,0:T(8,128)} custom-call(f32[47,128,256]{2,1,0:T(8,128)} %refs_0_.13, f32[46,128,256]{2,1,0:T(8,128)} %get-tuple-element.30.refs_1_, f32[2,128,256]{2,1,0:T(8,128)} %get-tuple-element.31.refs_2_, f32[2,128,256]{2,1,0:T(8,128)} %copy-done.7, f32[46,128,256]{2,1,0:T(8,128)} %refs_4_.13, ...), custom_call_target="tpu_custom_call", output_to_operand_aliasing={{}: (11, {})} | custom-call | flops 3221225472 | bytes 12582912 | tf_op jit(solution)/shard_map/pallas_call | solution.py:291
Async XLA Ops:
  292.0 33.9 %collective-permute-start.10 = (f32[8,128,256]{2,1,0:T(8,128)}, f32[8,128,256]{2,1,0:T(8,128)S(1)}, u32[]{:S(2)}, u32[]{:S(2)}) collective-permute-start(f32[8,128,256]{2,1,0:T(8,128)} %get-tuple-element.44.refs_2_), channel_id=1, source_target_pairs={{0,1},{1,0},{2,3},{3,2},{4,5},{5,4},{6,7},{7,6},{8,9},{9,8},{10,11... | collective-permute-start | bytes 3145736 | tf_op jit(solution)/shard_map/ppermute | solution.py:316
  292.6 34.9 %collective-permute-start.11 = (f32[8,128,256]{2,1,0:T(8,128)}, f32[8,128,256]{2,1,0:T(8,128)}, u32[]{:S(2)}, u32[]{:S(2)}) collective-permute-start(f32[8,128,256]{2,1,0:T(8,128)} %get-tuple-element.45.refs_5_), channel_id=1, source_target_pairs={{0,2},{1,3},{2,0},{3,1},{4,6},{5,7},{6,4},{7,5},{8,10},{9,11},{10,... | collective-permute-start | bytes 3145736 | tf_op jit(solution)/shard_map/ppermute | solution.py:317
  294.2 55.8 %collective-permute-start.8 = (f32[8,128,256]{2,1,0:T(8,128)}, f32[8,128,256]{2,1,0:T(8,128)}, u32[]{:S(2)}, u32[]{:S(2)}) collective-permute-start(f32[8,128,256]{2,1,0:T(8,128)} %get-tuple-element.42.refs_2_), channel_id=1, source_target_pairs={{0,1},{1,0},{2,3},{3,2},{4,5},{5,4},{6,7},{7,6},{8,9},{9,8},{10,11... | collective-permute-start | bytes 3145736 | tf_op jit(solution)/shard_map/ppermute | solution.py:316
  295.7 55.3 %collective-permute-start.9 = (f32[8,128,256]{2,1,0:T(8,128)}, f32[8,128,256]{2,1,0:T(8,128)}, u32[]{:S(2)}, u32[]{:S(2)}) collective-permute-start(f32[8,128,256]{2,1,0:T(8,128)} %get-tuple-element.43.refs_5_), channel_id=1, source_target_pairs={{0,2},{1,3},{2,0},{3,1},{4,6},{5,7},{6,4},{7,5},{8,10},{9,11},{10,... | collective-permute-start | bytes 3145736 | tf_op jit(solution)/shard_map/ppermute | solution.py:317
  296.2 76.0 %collective-permute-start.6 = (f32[8,128,256]{2,1,0:T(8,128)}, f32[8,128,256]{2,1,0:T(8,128)}, u32[]{:S(2)}, u32[]{:S(2)}) collective-permute-start(f32[8,128,256]{2,1,0:T(8,128)} %get-tuple-element.40.refs_2_), channel_id=1, source_target_pairs={{0,1},{1,0},{2,3},{3,2},{4,5},{5,4},{6,7},{7,6},{8,9},{9,8},{10,11... | collective-permute-start | bytes 3145736 | tf_op jit(solution)/shard_map/ppermute | solution.py:316
  305.2 20.8 %copy-start.2 = (f32[8,128,256]{2,1,0:T(8,128)S(1)}, f32[8,128,256]{2,1,0:T(8,128)}, u32[]{:S(2)}) copy-start(f32[8,128,256]{2,1,0:T(8,128)} %get-tuple-element.41.refs_5_) | copy-start | bytes 3145732
  305.2 22.4 %copy-start.1 = (f32[8,128,256]{2,1,0:T(8,128)S(1)}, f32[8,128,256]{2,1,0:T(8,128)}, u32[]{:S(2)}) copy-start(f32[8,128,256]{2,1,0:T(8,128)} %get-tuple-element.38.refs_2_) | copy-start | bytes 3145732
  326.0 1.6 copy-start.3
  326.0 47.4 %collective-permute-start.7 = (f32[8,128,256]{2,1,0:T(8,128)S(1)}, f32[8,128,256]{2,1,0:T(8,128)}, u32[]{:S(2)}, u32[]{:S(2)}) collective-permute-start(f32[8,128,256]{2,1,0:T(8,128)S(1)} %copy-done.2), channel_id=1, source_target_pairs={{0,2},{1,3},{2,0},{3,1},{4,6},{5,7},{6,4},{7,5},{8,10},{9,11},{10,... | collective-permute-start | bytes 3145736 | tf_op jit(solution)/shard_map/ppermute | solution.py:317
  327.6 22.4 %copy-start = (f32[8,128,256]{2,1,0:T(8,128)S(1)}, f32[8,128,256]{2,1,0:T(8,128)}, u32[]{:S(2)}) copy-start(f32[8,128,256]{2,1,0:T(8,128)} %get-tuple-element.39.refs_5_) | copy-start | bytes 3145732
  327.6 68.2 %collective-permute-start.4 = (f32[8,128,256]{2,1,0:T(8,128)S(1)}, f32[8,128,256]{2,1,0:T(8,128)}, u32[]{:S(2)}, u32[]{:S(2)}) collective-permute-start(f32[8,128,256]{2,1,0:T(8,128)S(1)} %copy-done.1), channel_id=1, source_target_pairs={{0,1},{1,0},{2,3},{3,2},{4,5},{5,4},{6,7},{7,6},{8,9},{9,8},{10,11... | collective-permute-start | bytes 3145736 | tf_op jit(solution)/shard_map/ppermute | solution.py:316
  350.0 46.7 %collective-permute-start.5 = (f32[8,128,256]{2,1,0:T(8,128)S(1)}, f32[8,128,256]{2,1,0:T(8,128)}, u32[]{:S(2)}, u32[]{:S(2)}) collective-permute-start(f32[8,128,256]{2,1,0:T(8,128)S(1)} %copy-done), channel_id=1, source_target_pairs={{0,2},{1,3},{2,0},{3,1},{4,6},{5,7},{6,4},{7,5},{8,10},{9,11},{10,... | collective-permute-start | bytes 3145736 | tf_op jit(solution)/shard_map/ppermute | solution.py:317
  350.9 21.2 %copy-start.4 = (f32[4,128,256]{2,1,0:T(8,128)S(1)}, f32[4,128,256]{2,1,0:T(8,128)}, u32[]{:S(2)}) copy-start(f32[4,128,256]{2,1,0:T(8,128)} %get-tuple-element.37.refs_5_) | copy-start | bytes 1572868
  350.9 22.5 %copy-start.6 = (f32[2,128,256]{2,1,0:T(8,128)S(1)}, f32[2,128,256]{2,1,0:T(8,128)}, u32[]{:S(2)}) copy-start(f32[2,128,256]{2,1,0:T(8,128)} %get-tuple-element.31.refs_2_) | copy-start | bytes 786436
  350.9 66.5 %collective-permute-start.2 = (f32[4,128,256]{2,1,0:T(8,128)}, f32[4,128,256]{2,1,0:T(8,128)}, u32[]{:S(2)}, u32[]{:S(2)}) collective-permute-start(f32[4,128,256]{2,1,0:T(8,128)} %get-tuple-element.36.refs_2_), channel_id=1, source_target_pairs={{0,1},{1,0},{2,3},{3,2},{4,5},{5,4},{6,7},{7,6},{8,9},{9,8},{10,11... | collective-permute-start | bytes 1572872 | tf_op jit(solution)/shard_map/ppermute | solution.py:316
  372.1 45.3 %collective-permute-start.3 = (f32[4,128,256]{2,1,0:T(8,128)S(1)}, f32[4,128,256]{2,1,0:T(8,128)}, u32[]{:S(2)}, u32[]{:S(2)}) collective-permute-start(f32[4,128,256]{2,1,0:T(8,128)S(1)} %copy-done.4), channel_id=1, source_target_pairs={{0,2},{1,3},{2,0},{3,1},{4,6},{5,7},{6,4},{7,5},{8,10},{9,11},{10,... | collective-permute-start | bytes 1572872 | tf_op jit(solution)/shard_map/ppermute | solution.py:317
  373.4 22.4 %copy-start.5 = (f32[2,128,256]{2,1,0:T(8,128)S(1)}, f32[2,128,256]{2,1,0:T(8,128)}, u32[]{:S(2)}) copy-start(f32[2,128,256]{2,1,0:T(8,128)} %get-tuple-element.32.refs_5_) | copy-start | bytes 786436
  373.4 57.3 %collective-permute-start = (f32[2,128,256]{2,1,0:T(8,128)S(1)}, f32[2,128,256]{2,1,0:T(8,128)S(1)}, u32[]{:S(2)}, u32[]{:S(2)}) collective-permute-start(f32[2,128,256]{2,1,0:T(8,128)S(1)} %copy-done.6), channel_id=1, source_target_pairs={{0,1},{1,0},{2,3},{3,2},{4,5},{5,4},{6,7},{7,6},{8,9},{9,8},{10,11... | collective-permute-start | bytes 786440 | tf_op jit(solution)/shard_map/ppermute | solution.py:316
  395.8 34.9 %collective-permute-start.1 = (f32[2,128,256]{2,1,0:T(8,128)S(1)}, f32[2,128,256]{2,1,0:T(8,128)S(1)}, u32[]{:S(2)}, u32[]{:S(2)}) collective-permute-start(f32[2,128,256]{2,1,0:T(8,128)S(1)} %copy-done.5), channel_id=1, source_target_pairs={{0,2},{1,3},{2,0},{3,1},{4,6},{5,7},{6,4},{7,5},{8,10},{9,11},{10,... | collective-permute-start | bytes 786440 | tf_op jit(solution)/shard_map/ppermute | solution.py:317
  430.7 0.7 copy-start.7
  431.4 0.7 copy-start.8

commit v2 on v1

--- a/solution.py
+++ b/solution.py
@@ -8,6 +8,7 @@
 
 HIGH = lax.Precision.HIGH
 MESH = pl.DeviceIdType.MESH
+STEP = 2
 STEPS = 4
 
 
@@ -32,10 +33,11 @@
 
 def solve_kernel(sizes, loads, first, second, inverses, *refs):
     count = len(sizes)
-    solved, (high, low, x1, y2, d1, d2) = refs[:2], refs[2:8]
-    x2, y1 = refs[8:8 + count], refs[8 + count:8 + 2 * count]
+    solved, (high, low, partial, x1, y2, d1, d2) = refs[:2], refs[2:9]
+    x2, y1 = refs[9:9 + count], refs[9 + count:9 + 2 * count]
     (inv, rhs, top, part, swapped, passed, block, high_stage, low_stage,
-     local_sem, link_send, link_recv, sum_send, sum_recv) = refs[8 + 2 * count:]
+     split_high, split_low,
+     local_sem, link_send, link_recv, sum_send, sum_recv) = refs[9 + 2 * count:]
     r, c = lax.axis_index("row"), lax.axis_index("col")
     z, core = r // 2, lax.rem(r, 2)
     chips = inv.shape[1] // inv.shape[2] // 2
@@ -73,17 +75,17 @@
     top_x = link(top.at[c], top.at[c], at=0, to=x_to)
     top_y = link(top.at[c], top.at[c], at=1, to=y_to)
     top_d = link(top.at[y_side], top.at[y_side], at=2, to=x_to)
-    total_blocks = sum(sizes)
-    send_x1 = link(first.at[pl.ds(1, total_blocks)], x1, at=3, to=x_to)
-    send_y2 = link(second, y2, at=4, to=y_to)
-    send_d1 = link(y1[0], d1, at=5, to=x_to)
-    send_d2 = link(x2[0], d2, at=6, to=y_to)
-    send_x2, send_y1 = [], []
-    start = 0
-    for k, size in enumerate(sizes):
-        send_x2.append(link(second.at[pl.ds(start, size)], x2[k], at=7 + k, to=x_to))
-        send_y1.append(link(first.at[pl.ds(start + 1, size)], y1[k], at=7 + count + k, to=y_to))
-        start += size
+    send_d1 = link(y1[0], d1, at=3, to=x_to)
+    send_d2 = link(x2[0], d2, at=4, to=y_to)
+    starts = [sum(sizes[:k]) for k in range(count)]
+    owned, send_x2, send_y1, send_x1, send_y2 = [], [], [], [], []
+    for k, (start, size) in enumerate(zip(starts, sizes)):
+        own1, own2 = first.at[pl.ds(start + 1, size)], second.at[pl.ds(start, size)]
+        owned.append((own1, own2))
+        send_x2.append(link(own2, x2[k], at=5 + 4 * k, to=x_to))
+        send_y1.append(link(own1, y1[k], at=6 + 4 * k, to=y_to))
+        send_x1.append(link(own1, x1.at[pl.ds(start, size)], at=7 + 4 * k, to=x_to))
+        send_y2.append(link(own2, y2.at[pl.ds(start, size)], at=8 + 4 * k, to=y_to))
     for copy in (top_x, top_y, send_x2[0], send_y1[0]):
         copy.start()
 
@@ -151,11 +153,11 @@
             h, l = halves(quarter)
             high_stage[j, k * width:(k + 1) * width] = h
             low_stage[j, k * width:(k + 1) * width] = l
-        depth = 4 * width
+        near, here = 3 * width, pl.ds(j * width, width)
         copies = [
             pltpu.make_async_copy(block.at[j], solved[j], local_sem.at[3 + 3 * j]),
-            pltpu.make_async_copy(high_stage.at[j], high.at[pl.ds(j * depth, depth)], local_sem.at[4 + 3 * j]),
-            pltpu.make_async_copy(low_stage.at[j], low.at[pl.ds(j * depth, depth)], local_sem.at[5 + 3 * j]),
+            pltpu.make_async_copy(high_stage.at[j, pl.ds(near, width)], high.at[here], local_sem.at[4 + 3 * j]),
+            pltpu.make_async_copy(low_stage.at[j, pl.ds(near, width)], low.at[here], local_sem.at[5 + 3 * j]),
         ]
         for copy in copies:
             copy.start()
@@ -168,12 +170,13 @@
     def forward_top():
         top_recv(y_side, 1)
         top_d.start()
-        for copy in send_x2[1:] + send_y1[1:]:
-            copy.start()
+        send_x1[0].start()
+        send_y2[0].start()
 
     def queue_rest():
-        send_x1.start()
-        send_y2.start()
+        for k in range(1, count):
+            for copy in (send_x2[k], send_y1[k], send_x1[k], send_y2[k]):
+                copy.start()
 
     def forward_first():
         send_y1[0].wait_recv()
@@ -199,14 +202,35 @@
     state = finish(1, nothing, forward_first)
     complete(1, state)
     copies += stage(1)
+
+    near = 3 * width
+
+    def step_body(*views):
+        loads_view, out_view = views[6:]
+        for at, piece in enumerate(views[:6]):
+            h, l = halves(piece[...].reshape(STEP * rows, width))
+            split_high[:, at * width:(at + 1) * width] = h
+            split_low[:, at * width:(at + 1) * width] = l
+        total = product((split_high[:, :near], split_low[:, :near]), (high_stage[0, :near], low_stage[0, :near]))
+        total = total + product((split_high[:, near:], split_low[:, near:]), (high_stage[1, :near], low_stage[1, :near]))
+        out_view[...] = loads_view[...] - total.reshape(STEP, rows, total.shape[1])
+
+    columns = rhs.shape[2]
+    narrow = pl.BlockSpec((STEP, rows, width), lambda i: (i, 0, 0))
+    wide = pl.BlockSpec((STEP, rows, columns), lambda i: (i, 0, 0))
+    for k, (start, size) in enumerate(zip(starts, sizes)):
+        here = pl.ds(start, size)
+        for copy in (send_x1[k], send_y2[k]) + ((send_x2[k], send_y1[k]) if k else ()):
+            copy.wait_recv()
+        pltpu.emit_pipeline(step_body, grid=(size // STEP,), in_specs=[narrow] * 6 + [wide], out_specs=[wide])(
+            owned[k][0], x1.at[here], y1[k], owned[k][1], x2[k], y2.at[here],
+            loads.at[pl.ds(start + 2, size)], partial.at[here])
     for copy in copies:
         copy.wait()
-    for copy in (top_x, top_y, top_d):
+    for copy in [top_x, top_y, top_d] + send_x1 + send_y1 + send_x2 + send_y2:
         copy.wait_send()
-    for copy in [send_x1, send_y2, send_d1, send_d2] + send_x2[1:] + send_y1[1:]:
+    for copy in (send_d1, send_d2):
         copy.wait()
-    for copy in (send_x2[0], send_y1[0]):
-        copy.wait_send()
 
 
 def solve(sizes, row_count, loads, first, second, inverses):
@@ -219,13 +243,14 @@
     shape = jax.ShapeDtypeStruct
     piece = lambda size: shape((size, rows, width), f32)
     pieces = [piece(size) for size in [sum(sizes)] * 2 + [sizes[0]] * 2 + list(sizes) * 2]
-    links = 7 + 2 * len(sizes)
+    links = 5 + 4 * len(sizes)
     sums = 2 * 4 * chips
     return pl.pallas_call(
         functools.partial(solve_kernel, sizes),
-        out_shape=[shape((depth, columns), f32)] * 2 + [shape((2 * depth, columns), bf16)] * 2 + pieces,
+        out_shape=[shape((depth, columns), f32)] * 2 + [shape((2 * width, columns), bf16)] * 2
+        + [shape((sum(sizes), rows, columns), f32)] + pieces,
         in_specs=[anywhere] * 4,
-        out_specs=[anywhere] * (4 + len(pieces)),
+        out_specs=[anywhere] * (5 + len(pieces)),
         scratch_shapes=[
             pltpu.VMEM((2, depth, rows), f32),
             pltpu.VMEM((2, rows, columns), f32),
@@ -236,6 +261,8 @@
             pltpu.VMEM((2, depth, columns), f32),
             pltpu.VMEM((2, depth, columns), bf16),
             pltpu.VMEM((2, depth, columns), bf16),
+            pltpu.VMEM((STEP * rows, 6 * width), bf16),
+            pltpu.VMEM((STEP * rows, 6 * width), bf16),
             pltpu.SemaphoreType.DMA((9,)),
             pltpu.SemaphoreType.DMA((links,)),
             pltpu.SemaphoreType.DMA((links,)),
@@ -264,21 +291,19 @@
         out[2 * at:2 * at + 2] = part[...] - total[2 * at:2 * at + 2]
 
 
-def update_chunk(firsts, seconds, loads, high, low, offset, size, previous):
-    rows, width = firsts[0][0].shape[1:]
+def update_chunk(pieces, loads, skip, high, low, offset, size, previous):
+    rows, width = pieces[0].shape[1:]
     columns = loads.shape[2]
     depth = high.shape[0]
-    count = loads.shape[0] - 2
+    count = loads.shape[0] - skip
     step = STEPS if size % STEPS == 0 and offset % STEPS == 0 else 2
     operands, in_specs = [], []
-    for array, at in firsts + seconds:
+    for array in pieces:
         operands.append(array)
-        in_specs.append(pl.BlockSpec(
-            (pl.Element(step), pl.Element(rows), pl.Element(width)),
-            lambda i, at=at: (at + i * step, 0, 0)))
+        in_specs.append(pl.BlockSpec((step, rows, width), lambda i: (i, 0, 0)))
     for k in range(step // 2):
         operands.append(loads)
-        in_specs.append(pl.BlockSpec((2, rows, columns), lambda i, k=k: (1 + (offset + i * step) // 2 + k, 0, 0)))
+        in_specs.append(pl.BlockSpec((2, rows, columns), lambda i, k=k: ((skip + offset + i * step) // 2 + k, 0, 0)))
     for factor in (high, low):
         operands.append(factor)
         in_specs.append(pl.BlockSpec((depth, columns), lambda i: (0, 0), pipeline_mode=pl.Buffered(1)))
@@ -289,7 +314,7 @@
         in_specs.append(pl.BlockSpec(memory_space=pl.ANY))
     work = size * rows * depth * columns
     return pl.pallas_call(
-        functools.partial(update_kernel, len(firsts + seconds), step),
+        functools.partial(update_kernel, len(pieces), step),
         out_shape=jax.ShapeDtypeStruct((count, rows, columns), jnp.float32),
         grid=(size // step,),
         in_specs=in_specs,
@@ -310,17 +335,15 @@
     along_x = [(c, c ^ 1) for c in range(4)]
     along_y = [(c, c ^ 2) for c in range(4)]
     results = solve(sizes, row_count, loads, below_first, below_second, inverses)
-    solved, (high, low, x1, y2, d1, d2) = results[:2], results[2:8]
-    x2, y1 = results[8:8 + len(sizes)], results[8 + len(sizes):]
+    solved, (high, low, partial, x1, y2, d1, d2) = results[:2], results[2:9]
+    x2, y1 = results[9:9 + len(sizes)], results[9 + len(sizes):]
     solved, high = lax.optimization_barrier((jnp.stack(solved), high))
     d1 = [d1] + [lax.ppermute(piece, "col", along_x) for piece in y1[1:]]
     d2 = [d2] + [lax.ppermute(piece, "col", along_y) for piece in x2[1:]]
     remaining = None
     at = 0
     for k, size in enumerate(sizes):
-        firsts = [(below_first, at + 1), (x1, at), (y1[k], 0), (d1[k], 0)]
-        seconds = [(below_second, at), (x2[k], 0), (y2, at), (d2[k], 0)]
-        remaining = update_chunk(firsts, seconds, loads, high, low, at, size, remaining)
+        remaining = update_chunk([d1[k], d2[k]], partial, 0, high, low, at, size, remaining)
         at += size
     return solved, remaining
 
@@ -339,9 +362,8 @@
     remaining = None
     at = 0
     for size in (count // 8 * 4, count - count // 8 * 4):
-        firsts = [(gather(below_first[at + 1:at + 1 + size]), 0)]
-        seconds = [(gather(below_second[at:at + size]), 0)]
-        remaining = update_chunk(firsts, seconds, loads, high, low, at, size, remaining)
+        pieces = [gather(below_first[at + 1:at + 1 + size]), gather(below_second[at:at + size])]
+        remaining = update_chunk(pieces, loads, 2, high, low, at, size, remaining)
         at += size
     return solved, remaining
 

time: 444 us -> 428 us (0.964)
  Pallas kernels: 417 us -> 354 us
  waiting for transfers between devices: 0.03 us -> 45.5 us
    pallas_call x7, Pallas kernels: 126 us -> 48.1 us  [update_chunk(): pl.pallas_call(functools.partial(update_kernel, len(pieces), step), out_s...]
    ppermute x6, waiting for transfers between devices: 0.02 us -> 44.9 us  [local_quarters(): d1 = [d1] + [lax.ppermute(piece, 'col', along_x) for piece in y1[1:]]]
    pallas_call x1, Pallas kernels: 291 us -> 306 us  [solve(): pl.pallas_call(functools.partial(solve_kernel, sizes), out_shape=[shape((...]
  transfers between devices with their start and end apart: 12 -> 12, of which waited for: 0 -> 5; matrix products, arithmetic and copies ran while one was open for 2% -> 2% of each run, Pallas kernels for 27% -> 10%
where the time goes in v2:
time: 428 us
  Pallas kernels  354 us (83%)
  waiting for transfers between devices  45.5 us (11%)
  starting transfers between devices  14.3 us (3%)
  other arithmetic  8.53 us (2%)
  local copies, waits for them, and re-layouts  5.21 us (1%)
    pallas_call x1, Pallas kernels, solve(): pl.pallas_call(functools.partial(solve_kernel, sizes), out_shape=[shape((...  306 us
    pallas_call x7, Pallas kernels, update_chunk(): pl.pallas_call(functools.partial(update_kernel, len(pieces), step), out_s...  48.1 us
    ppermute x6, waiting for transfers between devices, local_quarters(): d1 = [d1] + [lax.ppermute(piece, 'col', along_x) for piece in y1[1:]]  44.9 us
  transfers between devices with their start and end apart: 12, of which 5 were waited for; matrix products, arithmetic and copies ran while one was open for 2% of the time, Pallas kernels for 10%

profile of v2, /device:TPU:16, one launch (start us, length us, event | category | flops | bytes accessed | tf_op | source)
XLA Modules:
  0.0 428.1 jit_solution(7708065738220390156)
XLA Ops:
  0.6 305.7 %shard_map.59 = (f32[1024,1024]{1,0:T(8,128)}, f32[1024,1024]{1,0:T(8,128)}, bf16[512,1024]{1,0:T(8,128)(2,1)}, bf16[512,1024]{1,0:T(8,128)(2,1)}, f32[46,128,10...) custom-call(f32[48,128,1024]{2,1,0:T(8,128)} %loads.1, ...), custom_call_target="tpu_custom_call" | custom-call | tf_op jit(solution)/shard_map/pallas_call | solution.py:248
  306.4 1.6 collective-permute-start.8
  307.9 0.5 collective-permute-start.10
  308.5 1.5 collective-permute-start.11
  310.0 0.5 collective-permute-start.9
  310.5 1.5 collective-permute-start.6
  312.0 20.6 %collective-permute-done.8.refs_0_ = f32[8,128,256]{2,1,0:T(8,128)S(1)} collective-permute-done((f32[8,128,256]{2,1,0:T(8,128)}, f32[8,128,256]{2,1,0:T(8,128)S(1)}, u32[]{:S(2)}, u32[]{:S(2)}) %collective-permute-start.8) | collective-permute-done | bytes 1048608 | tf_op jit(solution)/shard_map/ppermute | solution.py:341
  332.6 0.0 copy-start.2
  332.6 1.5 collective-permute-start.7
  334.2 8.5 %pad_maximum_fusion = f32[2,1024,1024]{2,1,0:T(8,128)} fusion(f32[1,1024,1024]{2,1,0:T(8,128)} %bitcast.3, f32[1,1024,1024]{2,1,0:T(8,128)} %bitcast.2), kind=kLoop, calls=%fused_computation | loop fusion | flops 2097152 | bytes 16777216 | tf_op jit(solution)/shard_map/stack | solution.py:340
  342.7 0.0 copy-done.2
  342.7 12.4 %collective-permute-done.10.refs_0_ = f32[8,128,256]{2,1,0:T(8,128)S(1)} collective-permute-done((f32[8,128,256]{2,1,0:T(8,128)}, f32[8,128,256]{2,1,0:T(8,128)S(1)}, u32[]{:S(2)}, u32[]{:S(2)}) %collective-permute-start.10) | collective-permute-done | bytes 1048608 | tf_op jit(solution)/shard_map/ppermute | solution.py:341
  355.1 0.0 copy-start.4
  355.1 1.0 copy-done.4
  356.1 1.5 collective-permute-start.4
  357.6 0.0 collective-permute-done.11.refs_1_
  357.6 0.0 copy-start.5
  357.6 1.0 copy-done.5
  358.6 1.5 collective-permute-start.5
  360.1 7.6 %shard_map.60.refs_6_ = f32[46,128,1024]{2,1,0:T(8,128)} custom-call(f32[8,128,256]{2,1,0:T(8,128)} %get-tuple-element.42.refs_0_, f32[8,128,256]{2,1,0:T(8,128)} %get-tuple-element.43.refs_1_, f32[46,128,1024]{2,1,0:T(8,128)} %get-tuple-element.29.refs_2_.refs_3_, f32[46,128,1024]{2,1,0:T(8,128)} %get-tuple-element.29.refs_2_.refs_3_, ...), custom_call_target="tpu_custom_call" | custom-call | flops 3221225472 | bytes 12582912 | tf_op jit(solution)/shard_map/pallas_call | solution.py:316
  367.7 7.7 %shard_map.61.refs_6_ = f32[46,128,1024]{2,1,0:T(8,128)} custom-call(f32[8,128,256]{2,1,0:T(8,128)} %copy-done.4, f32[8,128,256]{2,1,0:T(8,128)} %copy-done.5, f32[46,128,1024]{2,1,0:T(8,128)} %get-tuple-element.29.refs_2_.refs_3_, f32[46,128,1024]{2,1,0:T(8,128)} %get-tuple-element.29.refs_2_.refs_3_, ...), custom_call_target="tpu_custom_call", output_to_operand_aliasing={{}: (6, {})} | custom-call | flops 3221225472 | bytes 12582912 | tf_op jit(solution)/shard_map/pallas_call | solution.py:316
  375.4 0.0 collective-permute-done.9.refs_1_
  375.4 0.6 collective-permute-start
  376.0 7.7 %shard_map.62.refs_6_ = f32[46,128,1024]{2,1,0:T(8,128)} custom-call(f32[8,128,256]{2,1,0:T(8,128)} %copy-done.2, f32[8,128,256]{2,1,0:T(8,128)} %collective-permute-done.9.refs_1_, f32[46,128,1024]{2,1,0:T(8,128)} %get-tuple-element.29.refs_2_.refs_3_, f32[46,128,1024]{2,1,0:T(8,128)} %get-tuple-element.29.refs_2_.refs_3_, ...), custom_call_target="tpu_custom_call", output_to_operand_aliasing={{}: (6, {})} | custom-call | flops 3221225472 | bytes 12582912 | tf_op jit(solution)/shard_map/pallas_call | solution.py:316
  383.7 0.0 collective-permute-done.6.refs_0_
  383.7 0.0 copy-start
  383.7 1.6 collective-permute-start.2
  385.3 0.0 collective-permute-done.7.refs_1_
  385.3 0.5 collective-permute-start.3
  385.8 0.0 copy-done
  385.8 7.9 %shard_map.63.refs_6_ = f32[46,128,1024]{2,1,0:T(8,128)} custom-call(f32[8,128,256]{2,1,0:T(8,128)} %copy-done, f32[8,128,256]{2,1,0:T(8,128)} %collective-permute-done.7.refs_1_, f32[46,128,1024]{2,1,0:T(8,128)} %get-tuple-element.29.refs_2_.refs_3_, f32[46,128,1024]{2,1,0:T(8,128)} %get-tuple-element.29.refs_2_.refs_3_, ...), custom_call_target="tpu_custom_call", output_to_operand_aliasing={{}: (6, {})} | custom-call | flops 3221225472 | bytes 12582912 | tf_op jit(solution)/shard_map/pallas_call | solution.py:316
  393.7 6.4 %collective-permute-done.4.refs_0_ = f32[8,128,256]{2,1,0:T(8,128)S(1)} collective-permute-done((f32[8,128,256]{2,1,0:T(8,128)}, f32[8,128,256]{2,1,0:T(8,128)S(1)}, u32[]{:S(2)}, u32[]{:S(2)}) %collective-permute-start.4) | collective-permute-done | bytes 1048608 | tf_op jit(solution)/shard_map/ppermute | solution.py:341
  400.1 0.0 copy-start.1
  400.1 1.5 collective-permute-start.1
  401.6 0.6 collective-permute-done.5.refs_1_
  402.2 0.0 copy-done.1
  402.2 0.0 copy-start.3
  402.2 1.1 copy-done.3
  403.2 7.6 %shard_map.64.refs_6_ = f32[46,128,1024]{2,1,0:T(8,128)} custom-call(f32[8,128,256]{2,1,0:T(8,128)} %copy-done.1, f32[8,128,256]{2,1,0:T(8,128)} %copy-done.3, f32[46,128,1024]{2,1,0:T(8,128)} %get-tuple-element.29.refs_2_.refs_3_, f32[46,128,1024]{2,1,0:T(8,128)} %get-tuple-element.29.refs_2_.refs_3_, ...), custom_call_target="tpu_custom_call", output_to_operand_aliasing={{}: (6, {})} | custom-call | flops 3221225472 | bytes 12582912 | tf_op jit(solution)/shard_map/pallas_call | solution.py:316
  410.9 5.5 %collective-permute-done.2.refs_0_ = f32[4,128,256]{2,1,0:T(8,128)S(1)} collective-permute-done((f32[4,128,256]{2,1,0:T(8,128)}, f32[4,128,256]{2,1,0:T(8,128)S(1)}, u32[]{:S(2)}, u32[]{:S(2)}) %collective-permute-start.2) | collective-permute-done | bytes 524320 | tf_op jit(solution)/shard_map/ppermute | solution.py:341
  416.4 0.0 copy-start.6
  416.4 0.0 collective-permute-done.3.refs_1_
  416.4 0.8 copy-done.6
  417.2 5.6 %shard_map.65.refs_5_ = f32[46,128,1024]{2,1,0:T(8,128)} custom-call(f32[4,128,256]{2,1,0:T(8,128)} %copy-done.6, f32[4,128,256]{2,1,0:T(8,128)} %collective-permute-done.3.refs_1_, f32[46,128,1024]{2,1,0:T(8,128)} %get-tuple-element.29.refs_2_.refs_3_, f32[46,128,1024]{2,1,0:T(8,128)} %get-tuple-element.29.refs_2_.refs_3_, ...), custom_call_target="tpu_custom_call", output_to_operand_aliasing={{}: (6, {})} | custom-call | flops 1610612736 | bytes 7340032 | tf_op jit(solution)/shard_map/pallas_call | solution.py:316
  422.8 0.0 collective-permute-done.refs_0_
  422.8 0.0 copy-start.7
  422.8 0.0 collective-permute-done.1.refs_1_
  422.8 0.7 copy-done.7
  423.5 0.0 copy-start.8
  423.5 0.7 copy-done.8
  424.1 4.0 shard_map.66
Async XLA Ops:
  306.4 26.3 %collective-permute-start.8 = (f32[8,128,256]{2,1,0:T(8,128)}, f32[8,128,256]{2,1,0:T(8,128)S(1)}, u32[]{:S(2)}, u32[]{:S(2)}) collective-permute-start(f32[8,128,256]{2,1,0:T(8,128)} %get-tuple-element.38), channel_id=1, source_target_pairs={{0,1},{1,0},{2,3},{3,2},{4,5},{5,4},{6,7},{7,6},{8,9},{9,8},{10,11... | collective-permute-start | bytes 3145736 | tf_op jit(solution)/shard_map/ppermute | solution.py:341
  307.9 47.2 %collective-permute-start.10 = (f32[8,128,256]{2,1,0:T(8,128)}, f32[8,128,256]{2,1,0:T(8,128)S(1)}, u32[]{:S(2)}, u32[]{:S(2)}) collective-permute-start(f32[8,128,256]{2,1,0:T(8,128)} %get-tuple-element.40), channel_id=1, source_target_pairs={{0,1},{1,0},{2,3},{3,2},{4,5},{5,4},{6,7},{7,6},{8,9},{9,8},{10,11... | collective-permute-start | bytes 3145736 | tf_op jit(solution)/shard_map/ppermute | solution.py:341
  308.5 49.1 %collective-permute-start.11 = (f32[8,128,256]{2,1,0:T(8,128)}, f32[8,128,256]{2,1,0:T(8,128)S(1)}, u32[]{:S(2)}, u32[]{:S(2)}) collective-permute-start(f32[8,128,256]{2,1,0:T(8,128)} %get-tuple-element.41), channel_id=1, source_target_pairs={{0,2},{1,3},{2,0},{3,1},{4,6},{5,7},{6,4},{7,5},{8,10},{9,11},{10,... | collective-permute-start | bytes 3145736 | tf_op jit(solution)/shard_map/ppermute | solution.py:342
  310.0 65.4 %collective-permute-start.9 = (f32[8,128,256]{2,1,0:T(8,128)}, f32[8,128,256]{2,1,0:T(8,128)}, u32[]{:S(2)}, u32[]{:S(2)}) collective-permute-start(f32[8,128,256]{2,1,0:T(8,128)} %get-tuple-element.39), channel_id=1, source_target_pairs={{0,2},{1,3},{2,0},{3,1},{4,6},{5,7},{6,4},{7,5},{8,10},{9,11},{10,... | collective-permute-start | bytes 3145736 | tf_op jit(solution)/shard_map/ppermute | solution.py:342
  310.5 73.2 %collective-permute-start.6 = (f32[8,128,256]{2,1,0:T(8,128)}, f32[8,128,256]{2,1,0:T(8,128)S(1)}, u32[]{:S(2)}, u32[]{:S(2)}) collective-permute-start(f32[8,128,256]{2,1,0:T(8,128)} %get-tuple-element.36), channel_id=1, source_target_pairs={{0,1},{1,0},{2,3},{3,2},{4,5},{5,4},{6,7},{7,6},{8,9},{9,8},{10,11... | collective-permute-start | bytes 3145736 | tf_op jit(solution)/shard_map/ppermute | solution.py:341
  332.6 10.0 %copy-start.2 = (f32[8,128,256]{2,1,0:T(8,128)}, f32[8,128,256]{2,1,0:T(8,128)S(1)}, u32[]{:S(2)}) copy-start(f32[8,128,256]{2,1,0:T(8,128)S(1)} %collective-permute-done.8.refs_0_) | copy-start | bytes 3145732
  332.6 52.6 %collective-permute-start.7 = (f32[8,128,256]{2,1,0:T(8,128)}, f32[8,128,256]{2,1,0:T(8,128)}, u32[]{:S(2)}, u32[]{:S(2)}) collective-permute-start(f32[8,128,256]{2,1,0:T(8,128)} %get-tuple-element.37), channel_id=1, source_target_pairs={{0,2},{1,3},{2,0},{3,1},{4,6},{5,7},{6,4},{7,5},{8,10},{9,11},{10,... | collective-permute-start | bytes 3145736 | tf_op jit(solution)/shard_map/ppermute | solution.py:342
  355.1 1.0 copy-start.4
  356.1 44.0 %collective-permute-start.4 = (f32[8,128,256]{2,1,0:T(8,128)}, f32[8,128,256]{2,1,0:T(8,128)S(1)}, u32[]{:S(2)}, u32[]{:S(2)}) collective-permute-start(f32[8,128,256]{2,1,0:T(8,128)} %get-tuple-element.34), channel_id=1, source_target_pairs={{0,1},{1,0},{2,3},{3,2},{4,5},{5,4},{6,7},{7,6},{8,9},{9,8},{10,11... | collective-permute-start | bytes 3145736 | tf_op jit(solution)/shard_map/ppermute | solution.py:341
  357.6 1.0 copy-start.5
  358.6 43.6 %collective-permute-start.5 = (f32[8,128,256]{2,1,0:T(8,128)}, f32[8,128,256]{2,1,0:T(8,128)S(1)}, u32[]{:S(2)}, u32[]{:S(2)}) collective-permute-start(f32[8,128,256]{2,1,0:T(8,128)} %get-tuple-element.35), channel_id=1, source_target_pairs={{0,2},{1,3},{2,0},{3,1},{4,6},{5,7},{6,4},{7,5},{8,10},{9,11},{10,... | collective-permute-start | bytes 3145736 | tf_op jit(solution)/shard_map/ppermute | solution.py:342
  375.4 47.4 %collective-permute-start = (f32[2,128,256]{2,1,0:T(8,128)}, f32[2,128,256]{2,1,0:T(8,128)S(1)}, u32[]{:S(2)}, u32[]{:S(2)}) collective-permute-start(f32[2,128,256]{2,1,0:T(8,128)} %get-tuple-element.27), channel_id=1, source_target_pairs={{0,1},{1,0},{2,3},{3,2},{4,5},{5,4},{6,7},{7,6},{8,9},{9,8},{10,11... | collective-permute-start | bytes 786440 | tf_op jit(solution)/shard_map/ppermute | solution.py:341
  383.7 2.1 copy-start
  383.7 32.6 %collective-permute-start.2 = (f32[4,128,256]{2,1,0:T(8,128)}, f32[4,128,256]{2,1,0:T(8,128)S(1)}, u32[]{:S(2)}, u32[]{:S(2)}) collective-permute-start(f32[4,128,256]{2,1,0:T(8,128)} %get-tuple-element.32), channel_id=1, source_target_pairs={{0,1},{1,0},{2,3},{3,2},{4,5},{5,4},{6,7},{7,6},{8,9},{9,8},{10,11... | collective-permute-start | bytes 1572872 | tf_op jit(solution)/shard_map/ppermute | solution.py:341
  385.3 31.1 %collective-permute-start.3 = (f32[4,128,256]{2,1,0:T(8,128)}, f32[4,128,256]{2,1,0:T(8,128)}, u32[]{:S(2)}, u32[]{:S(2)}) collective-permute-start(f32[4,128,256]{2,1,0:T(8,128)} %get-tuple-element.33), channel_id=1, source_target_pairs={{0,2},{1,3},{2,0},{3,1},{4,6},{5,7},{6,4},{7,5},{8,10},{9,11},{10,... | collective-permute-start | bytes 1572872 | tf_op jit(solution)/shard_map/ppermute | solution.py:342
  400.1 2.1 copy-start.1
  400.1 22.7 %collective-permute-start.1 = (f32[2,128,256]{2,1,0:T(8,128)}, f32[2,128,256]{2,1,0:T(8,128)S(1)}, u32[]{:S(2)}, u32[]{:S(2)}) collective-permute-start(f32[2,128,256]{2,1,0:T(8,128)} %get-tuple-element.28), channel_id=1, source_target_pairs={{0,2},{1,3},{2,0},{3,1},{4,6},{5,7},{6,4},{7,5},{8,10},{9,11},{10,... | collective-permute-start | bytes 786440 | tf_op jit(solution)/shard_map/ppermute | solution.py:342
  402.2 1.1 copy-start.3
  416.4 0.8 copy-start.6
  422.8 0.7 copy-start.7
  423.5 0.7 copy-start.8

commit v3 on v2

--- a/solution.py
+++ b/solution.py
@@ -13,12 +13,11 @@
 
 
 def chunk_sizes(count):
-    sizes = []
-    for size in (8, 4, 2):
-        while count - size >= size // 2:
-            sizes.append(size)
-            count -= size
-    return sizes + [count] if count else sizes
+    first, last = count // 10 * 2, count // 20 * 2
+    middle = count - first - last
+    parts = -(-middle // 12)
+    at = [k * middle // (2 * parts) * 2 for k in range(parts)] + [middle]
+    return [first] + [after - before for before, after in zip(at, at[1:])] + [last]
 
 
 def halves(value):
@@ -33,11 +32,11 @@
 
 def solve_kernel(sizes, loads, first, second, inverses, *refs):
     count = len(sizes)
-    solved, (high, low, partial, x1, y2, d1, d2) = refs[:2], refs[2:9]
-    x2, y1 = refs[9:9 + count], refs[9 + count:9 + 2 * count]
+    solved, (high, low, far_high, far_low, partial, x1, y2, d1, d2) = refs[:2], refs[2:11]
+    x2, y1 = refs[11:11 + count], refs[11 + count:11 + 2 * count]
     (inv, rhs, top, part, swapped, passed, block, high_stage, low_stage,
      split_high, split_low,
-     local_sem, link_send, link_recv, sum_send, sum_recv) = refs[9 + 2 * count:]
+     local_sem, link_send, link_recv, sum_send, sum_recv) = refs[11 + 2 * count:]
     r, c = lax.axis_index("row"), lax.axis_index("col")
     z, core = r // 2, lax.rem(r, 2)
     chips = inv.shape[1] // inv.shape[2] // 2
@@ -153,12 +152,15 @@
             h, l = halves(quarter)
             high_stage[j, k * width:(k + 1) * width] = h
             low_stage[j, k * width:(k + 1) * width] = l
-        near, here = 3 * width, pl.ds(j * width, width)
-        copies = [
-            pltpu.make_async_copy(block.at[j], solved[j], local_sem.at[3 + 3 * j]),
-            pltpu.make_async_copy(high_stage.at[j, pl.ds(near, width)], high.at[here], local_sem.at[4 + 3 * j]),
-            pltpu.make_async_copy(low_stage.at[j, pl.ds(near, width)], low.at[here], local_sem.at[5 + 3 * j]),
+        near, here, whole = 3 * width, pl.ds(j * width, width), pl.ds(j * 4 * width, 4 * width)
+        moves = [
+            (block.at[j], solved[j]),
+            (high_stage.at[j], high.at[whole]),
+            (low_stage.at[j], low.at[whole]),
+            (high_stage.at[j, pl.ds(near, width)], far_high.at[here]),
+            (low_stage.at[j, pl.ds(near, width)], far_low.at[here]),
         ]
+        copies = [pltpu.make_async_copy(src, dst, local_sem.at[3 + 5 * j + k]) for k, (src, dst) in enumerate(moves)]
         for copy in copies:
             copy.start()
         return copies
@@ -222,6 +224,8 @@
         here = pl.ds(start, size)
         for copy in (send_x1[k], send_y2[k]) + ((send_x2[k], send_y1[k]) if k else ()):
             copy.wait_recv()
+        if k == 0:
+            continue
         pltpu.emit_pipeline(step_body, grid=(size // STEP,), in_specs=[narrow] * 6 + [wide], out_specs=[wide])(
             owned[k][0], x1.at[here], y1[k], owned[k][1], x2[k], y2.at[here],
             loads.at[pl.ds(start + 2, size)], partial.at[here])
@@ -247,10 +251,11 @@
     sums = 2 * 4 * chips
     return pl.pallas_call(
         functools.partial(solve_kernel, sizes),
-        out_shape=[shape((depth, columns), f32)] * 2 + [shape((2 * width, columns), bf16)] * 2
+        out_shape=[shape((depth, columns), f32)] * 2 + [shape((2 * depth, columns), bf16)] * 2
+        + [shape((2 * width, columns), bf16)] * 2
         + [shape((sum(sizes), rows, columns), f32)] + pieces,
         in_specs=[anywhere] * 4,
-        out_specs=[anywhere] * (5 + len(pieces)),
+        out_specs=[anywhere] * (7 + len(pieces)),
         scratch_shapes=[
             pltpu.VMEM((2, depth, rows), f32),
             pltpu.VMEM((2, rows, columns), f32),
@@ -263,7 +268,7 @@
             pltpu.VMEM((2, depth, columns), bf16),
             pltpu.VMEM((STEP * rows, 6 * width), bf16),
             pltpu.VMEM((STEP * rows, 6 * width), bf16),
-            pltpu.SemaphoreType.DMA((9,)),
+            pltpu.SemaphoreType.DMA((13,)),
             pltpu.SemaphoreType.DMA((links,)),
             pltpu.SemaphoreType.DMA((links,)),
             pltpu.SemaphoreType.DMA((sums,)),
@@ -292,15 +297,17 @@
 
 
 def update_chunk(pieces, loads, skip, high, low, offset, size, previous):
-    rows, width = pieces[0].shape[1:]
+    rows, width = pieces[0][0].shape[1:]
     columns = loads.shape[2]
     depth = high.shape[0]
     count = loads.shape[0] - skip
     step = STEPS if size % STEPS == 0 and offset % STEPS == 0 else 2
     operands, in_specs = [], []
-    for array in pieces:
+    for array, at in pieces:
         operands.append(array)
-        in_specs.append(pl.BlockSpec((step, rows, width), lambda i: (i, 0, 0)))
+        in_specs.append(pl.BlockSpec(
+            (pl.Element(step), pl.Element(rows), pl.Element(width)),
+            lambda i, at=at: (at + i * step, 0, 0)))
     for k in range(step // 2):
         operands.append(loads)
         in_specs.append(pl.BlockSpec((2, rows, columns), lambda i, k=k: ((skip + offset + i * step) // 2 + k, 0, 0)))
@@ -335,16 +342,24 @@
     along_x = [(c, c ^ 1) for c in range(4)]
     along_y = [(c, c ^ 2) for c in range(4)]
     results = solve(sizes, row_count, loads, below_first, below_second, inverses)
-    solved, (high, low, partial, x1, y2, d1, d2) = results[:2], results[2:9]
-    x2, y1 = results[9:9 + len(sizes)], results[9 + len(sizes):]
-    solved, high = lax.optimization_barrier((jnp.stack(solved), high))
-    d1 = [d1] + [lax.ppermute(piece, "col", along_x) for piece in y1[1:]]
-    d2 = [d2] + [lax.ppermute(piece, "col", along_y) for piece in x2[1:]]
-    remaining = None
-    at = 0
-    for k, size in enumerate(sizes):
-        remaining = update_chunk([d1[k], d2[k]], partial, 0, high, low, at, size, remaining)
-        at += size
+    solved, (high, low, far_high, far_low, partial, x1, y2, d1, d2) = results[:2], results[2:11]
+    x2, y1 = results[11:11 + len(sizes)], results[11 + len(sizes):]
+    pieces = [(below_first, 1), (x1, 0), (y1[0], 0), (d1, 0), (below_second, 0), (x2[0], 0), (y2, 0), (d2, 0)]
+    remaining = update_chunk(pieces, loads, 2, high, low, 0, sizes[0], None)
+    solved, far_high = lax.optimization_barrier((jnp.stack(solved), far_high))
+    far1, far2 = {}, {}
+    for k in range(1, len(sizes)):
+        near1, near2 = y1[k], x2[k]
+        if k > 2:
+            near1, far1[k - 2] = lax.optimization_barrier((near1, far1[k - 2]))
+            near2, far2[k - 2] = lax.optimization_barrier((near2, far2[k - 2]))
+        far1[k] = lax.ppermute(near1, "col", along_x)
+        far2[k] = lax.ppermute(near2, "col", along_y)
+    at = sizes[0]
+    for k in range(1, len(sizes)):
+        chunk = [(far1[k], 0), (far2[k], 0)]
+        remaining = update_chunk(chunk, partial, 0, far_high, far_low, at, sizes[k], remaining)
+        at += sizes[k]
     return solved, remaining
 
 
@@ -362,7 +377,7 @@
     remaining = None
     at = 0
     for size in (count // 8 * 4, count - count // 8 * 4):
-        pieces = [gather(below_first[at + 1:at + 1 + size]), gather(below_second[at:at + size])]
+        pieces = [(gather(below_first[at + 1:at + 1 + size]), 0), (gather(below_second[at:at + size]), 0)]
         remaining = update_chunk(pieces, loads, 2, high, low, at, size, remaining)
         at += size
     return solved, remaining

time: 428 us -> 413 us (0.965)
  starting transfers between devices: 14.3 us -> 8.98 us
  Pallas kernels: 354 us -> 349 us
  local copies, waits for them, and re-layouts: 5.21 us -> 0.81 us
    pallas_call x1, Pallas kernels: 306 us -> 291 us  [solve(): pl.pallas_call(functools.partial(solve_kernel, sizes), out_shape=[shape((...]
    pallas_call x7 -> x5, Pallas kernels: 48.1 us -> 57 us  [update_chunk(): pl.pallas_call(functools.partial(update_kernel, len(pieces), step), out_s...]
    ppermute x12 -> x8, starting transfers between devices: 14.3 us -> 8.98 us  [the longest x4 4.79 us: local_quarters(): far2[k] = lax.ppermute(near2, 'col', along_y)]
    unnamed x18 -> x6, local copies, waits for them, and re-layouts: 5.21 us -> 0.81 us
    ppermute x12 -> x8, waiting for transfers between devices: 45.5 us -> 41.4 us  [the longest x4 22 us: local_quarters(): far2[k] = lax.ppermute(near2, 'col', along_y)]
  transfers between devices with their start and end apart: 12 -> 8, of which waited for: 5 -> 3; matrix products, arithmetic and copies ran while one was open for 2% -> 2% of each run, Pallas kernels for 10% -> 13%
where the time goes in v3:
time: 413 us; the launch traced here: 409 us
  Pallas kernels  349 us (85%)
  waiting for transfers between devices  41.4 us (10%)
  starting transfers between devices  8.98 us (2%)
  other arithmetic  8.53 us (2%)
    pallas_call x1, Pallas kernels, solve(): pl.pallas_call(functools.partial(solve_kernel, sizes), out_shape=[shape((...  291 us
    pallas_call x5, Pallas kernels, update_chunk(): pl.pallas_call(functools.partial(update_kernel, len(pieces), step), out_s...  57 us
    ppermute x4, waiting for transfers between devices, local_quarters(): far2[k] = lax.ppermute(near2, 'col', along_y)  22 us
    ppermute x4, waiting for transfers between devices, local_quarters(): far1[k] = lax.ppermute(near1, 'col', along_x)  19.5 us
    another operation x1, other arithmetic, local_quarters(): solved, far_high = lax.optimization_barrier((jnp.stack(solved), far_high))  8.53 us
  transfers between devices with their start and end apart: 8, of which 3 were waited for; matrix products, arithmetic and copies ran while one was open for 2% of the time, Pallas kernels for 13%

profile of v3, /device:TPU:16, one launch (start us, length us, event | category | flops | bytes accessed | tf_op | source)
XLA Modules:
  0.0 408.9 jit_solution(11785990971928317450)
XLA Ops:
  0.6 291.5 %shard_map.59 = (f32[1024,1024]{1,0:T(8,128)}, f32[1024,1024]{1,0:T(8,128)}, bf16[2048,1024]{1,0:T(8,128)(2,1)}, bf16[2048,1024]{1,0:T(8,128)(2,1)}, bf16[512,10...) custom-call(f32[48,128,1024]{2,1,0:T(8,128)} %refs_9_.1, ...), custom_call_target="tpu_custom_call" | custom-call | tf_op jit(solution)/shard_map/pallas_call | solution.py:252
  292.1 0.6 collective-permute-start.4
  292.7 1.5 collective-permute-start.6
  294.2 1.5 collective-permute-start
  295.7 0.5 collective-permute-start.2
  296.2 8.5 %pad_maximum_fusion = f32[2,1024,1024]{2,1,0:T(8,128)} fusion(f32[1,1024,1024]{2,1,0:T(8,128)} %bitcast.3, f32[1,1024,1024]{2,1,0:T(8,128)} %bitcast.2), kind=kLoop, calls=%fused_computation | loop fusion | flops 2097152 | bytes 16777216 | tf_op jit(solution)/shard_map/stack | solution.py:349
  304.8 19.4 %collective-permute-done.4.refs_0_ = f32[10,128,256]{2,1,0:T(8,128)} collective-permute-done((f32[10,128,256]{2,1,0:T(8,128)}, f32[10,128,256]{2,1,0:T(8,128)}, u32[]{:S(2)}, u32[]{:S(2)}) %collective-permute-start.4) | collective-permute-done | bytes 1310752 | tf_op jit(solution)/shard_map/ppermute | solution.py:356
  324.2 0.5 collective-permute-done.6.refs_1_
  324.7 1.5 collective-permute-start.7
  326.3 1.5 collective-permute-start.5
  327.8 20.6 %shard_map.60.refs_5_ = f32[46,128,1024]{2,1,0:T(8,128)} custom-call(f32[47,128,256]{2,1,0:T(8,128)} %refs_0_.1, f32[46,128,256]{2,1,0:T(8,128)} %get-tuple-element.56.refs_1_, f32[8,128,256]{2,1,0:T(8,128)} %get-tuple-element.57.refs_2_, f32[8,128,256]{2,1,0:T(8,128)} %get-tuple-element.58.refs_3_, f32[46,128,256]{2,1,0:T(8,128)} %refs_4_.1, ...), custom_call_target="tpu_custom_call" | custom-call | flops 12884901888 | bytes 25165824 | tf_op jit(solution)/shard_map/pallas_call | solution.py:323
  348.4 9.6 %shard_map.61.refs_5_ = f32[46,128,1024]{2,1,0:T(8,128)} custom-call(f32[10,128,256]{2,1,0:T(8,128)} %collective-permute-done.4.refs_0_, f32[10,128,256]{2,1,0:T(8,128)} %collective-permute-done.6.refs_1_, f32[46,128,1024]{2,1,0:T(8,128)} %get-tuple-element.43.refs_2_, bf16[512,1024]{1,0:T(8,128)(2,1)} %get-tuple-element.44.refs_3_, ...), custom_call_target="tpu_custom_call", output_to_operand_aliasing={{}: (5, {})} | custom-call | flops 4026531840 | bytes 15204352 | tf_op jit(solution)/shard_map/pallas_call | solution.py:323
  358.0 0.0 collective-permute-done.refs_0_
  358.0 0.0 copy-start
  358.0 0.6 collective-permute-start.1
  358.6 0.0 collective-permute-done.2.refs_1_
  358.6 0.0 copy-start.1
  358.6 1.2 collective-permute-start.3
  359.9 0.0 copy-done
  359.9 0.0 copy-done.1
  359.9 10.8 %shard_map.62.refs_5_ = f32[46,128,1024]{2,1,0:T(8,128)} custom-call(f32[12,128,256]{2,1,0:T(8,128)} %copy-done, f32[12,128,256]{2,1,0:T(8,128)} %copy-done.1, f32[46,128,1024]{2,1,0:T(8,128)} %get-tuple-element.43.refs_2_, bf16[512,1024]{1,0:T(8,128)(2,1)} %get-tuple-element.44.refs_3_, ...), custom_call_target="tpu_custom_call", output_to_operand_aliasing={{}: (5, {})} | custom-call | flops 4831838208 | bytes 17825792 | tf_op jit(solution)/shard_map/pallas_call | solution.py:323
  370.7 21.4 %collective-permute-done.7.refs_1_ = f32[12,128,256]{2,1,0:T(8,128)} collective-permute-done((f32[12,128,256]{2,1,0:T(8,128)}, f32[12,128,256]{2,1,0:T(8,128)}, u32[]{:S(2)}, u32[]{:S(2)}) %collective-permute-start.7) | collective-permute-done | bytes 1572896 | tf_op jit(solution)/shard_map/ppermute | solution.py:357
  392.2 0.0 collective-permute-done.5.refs_0_
  392.2 10.8 %shard_map.63.refs_5_ = f32[46,128,1024]{2,1,0:T(8,128)} custom-call(f32[12,128,256]{2,1,0:T(8,128)} %collective-permute-done.5.refs_0_, f32[12,128,256]{2,1,0:T(8,128)} %collective-permute-done.7.refs_1_, f32[46,128,1024]{2,1,0:T(8,128)} %get-tuple-element.43.refs_2_, bf16[512,1024]{1,0:T(8,128)(2,1)} %get-tuple-element.44.refs_3_, ...), custom_call_target="tpu_custom_call", output_to_operand_aliasing={{}: (5, {})} | custom-call | flops 4831838208 | bytes 17825792 | tf_op jit(solution)/shard_map/pallas_call | solution.py:323
  403.0 0.0 collective-permute-done.1.refs_0_
  403.0 0.0 copy-start.2
  403.0 0.0 collective-permute-done.3.refs_1_
  403.0 0.8 copy-done.2
  403.8 5.1 %shard_map.64 = f32[46,128,1024]{2,1,0:T(8,128)} custom-call(f32[4,128,256]{2,1,0:T(8,128)} %copy-done.2, f32[4,128,256]{2,1,0:T(8,128)} %collective-permute-done.3.refs_1_, f32[46,128,1024]{2,1,0:T(8,128)} %get-tuple-element.43.refs_2_, bf16[512,1024]{1,0:T(8,128)(2,1)} %get-tuple-element.44.refs_3_, ...), custom_call_target="tpu_custom_call", output_to_operand_aliasing={{}: (5, {})} | custom-call | flops 1610612736 | bytes 7340032 | tf_op jit(solution)/shard_map/pallas_call | solution.py:323
Async XLA Ops:
  292.1 32.1 %collective-permute-start.4 = (f32[10,128,256]{2,1,0:T(8,128)}, f32[10,128,256]{2,1,0:T(8,128)}, u32[]{:S(2)}, u32[]{:S(2)}) collective-permute-start(f32[10,128,256]{2,1,0:T(8,128)} %get-tuple-element.47), channel_id=1, source_target_pairs={{0,1},{1,0},{2,3},{3,2},{4,5},{5,4},{6,7},{7,6},{8,9},{9,8},{10,11... | collective-permute-start | bytes 3932168 | tf_op jit(solution)/shard_map/ppermute | solution.py:356
  292.7 32.0 %collective-permute-start.6 = (f32[10,128,256]{2,1,0:T(8,128)}, f32[10,128,256]{2,1,0:T(8,128)}, u32[]{:S(2)}, u32[]{:S(2)}) collective-permute-start(f32[10,128,256]{2,1,0:T(8,128)} %get-tuple-element.50), channel_id=1, source_target_pairs={{0,2},{1,3},{2,0},{3,1},{4,6},{5,7},{6,4},{7,5},{8,10},{9,11},{10,... | collective-permute-start | bytes 3932168 | tf_op jit(solution)/shard_map/ppermute | solution.py:357
  294.2 63.8 %collective-permute-start = (f32[12,128,256]{2,1,0:T(8,128)}, f32[12,128,256]{2,1,0:T(8,128)S(1)}, u32[]{:S(2)}, u32[]{:S(2)}) collective-permute-start(f32[12,128,256]{2,1,0:T(8,128)} %get-tuple-element.38), channel_id=1, source_target_pairs={{0,1},{1,0},{2,3},{3,2},{4,5},{5,4},{6,7},{7,6},{8,9},{9,8},{10,11... | collective-permute-start | bytes 4718600 | tf_op jit(solution)/shard_map/ppermute | solution.py:356
  295.7 62.9 %collective-permute-start.2 = (f32[12,128,256]{2,1,0:T(8,128)}, f32[12,128,256]{2,1,0:T(8,128)S(1)}, u32[]{:S(2)}, u32[]{:S(2)}) collective-permute-start(f32[12,128,256]{2,1,0:T(8,128)} %get-tuple-element.41), channel_id=1, source_target_pairs={{0,2},{1,3},{2,0},{3,1},{4,6},{5,7},{6,4},{7,5},{8,10},{9,11},{10,... | collective-permute-start | bytes 4718600 | tf_op jit(solution)/shard_map/ppermute | solution.py:357
  324.7 67.4 %collective-permute-start.7 = (f32[12,128,256]{2,1,0:T(8,128)}, f32[12,128,256]{2,1,0:T(8,128)}, u32[]{:S(2)}, u32[]{:S(2)}) collective-permute-start(f32[12,128,256]{2,1,0:T(8,128)} %get-tuple-element.51), channel_id=1, source_target_pairs={{0,2},{1,3},{2,0},{3,1},{4,6},{5,7},{6,4},{7,5},{8,10},{9,11},{10,... | collective-permute-start | bytes 4718600 | tf_op jit(solution)/shard_map/ppermute | solution.py:357
  326.3 65.9 %collective-permute-start.5 = (f32[12,128,256]{2,1,0:T(8,128)}, f32[12,128,256]{2,1,0:T(8,128)}, u32[]{:S(2)}, u32[]{:S(2)}) collective-permute-start(f32[12,128,256]{2,1,0:T(8,128)} %get-tuple-element.48), channel_id=1, source_target_pairs={{0,1},{1,0},{2,3},{3,2},{4,5},{5,4},{6,7},{7,6},{8,9},{9,8},{10,11... | collective-permute-start | bytes 4718600 | tf_op jit(solution)/shard_map/ppermute | solution.py:356
  358.0 1.9 copy-start
  358.0 45.0 %collective-permute-start.1 = (f32[4,128,256]{2,1,0:T(8,128)}, f32[4,128,256]{2,1,0:T(8,128)S(1)}, u32[]{:S(2)}, u32[]{:S(2)}) collective-permute-start(f32[4,128,256]{2,1,0:T(8,128)} %get-tuple-element.39), channel_id=1, source_target_pairs={{0,1},{1,0},{2,3},{3,2},{4,5},{5,4},{6,7},{7,6},{8,9},{9,8},{10,11... | collective-permute-start | bytes 1572872 | tf_op jit(solution)/shard_map/ppermute | solution.py:356
  358.6 1.3 copy-start.1
  358.6 44.4 %collective-permute-start.3 = (f32[4,128,256]{2,1,0:T(8,128)}, f32[4,128,256]{2,1,0:T(8,128)}, u32[]{:S(2)}, u32[]{:S(2)}) collective-permute-start(f32[4,128,256]{2,1,0:T(8,128)} %get-tuple-element.42), channel_id=1, source_target_pairs={{0,2},{1,3},{2,0},{3,1},{4,6},{5,7},{6,4},{7,5},{8,10},{9,11},{10,... | collective-permute-start | bytes 1572872 | tf_op jit(solution)/shard_map/ppermute | solution.py:357
  403.0 0.8 copy-start.2

commit v4 on v3

--- a/solution.py
+++ b/solution.py
@@ -69,11 +69,13 @@
         pl.semaphore_signal(barrier, inc=1, device_id=to, device_id_type=MESH)
     pl.semaphore_wait(barrier, len(partners))
 
-    top_in.wait()
     link = functools.partial(remote, sends=link_send, recvs=link_recv)
-    top_x = link(top.at[c], top.at[c], at=0, to=x_to)
-    top_y = link(top.at[c], top.at[c], at=1, to=y_to)
-    top_d = link(top.at[y_side], top.at[y_side], at=2, to=x_to)
+    upper, lower = pl.ds(0, rows // 2), pl.ds(rows // 2, rows - rows // 2)
+    last_link = 5 + 4 * count
+    top_x = link(first.at[0], top.at[c], at=0, to=x_to)
+    top_y = link(first.at[0], top.at[c], at=1, to=y_to)
+    top_d1 = link(top.at[y_side, upper], top.at[y_side, upper], at=2, to=x_to)
+    top_d2 = link(top.at[x_side, lower], top.at[x_side, lower], at=last_link, to=y_to)
     send_d1 = link(y1[0], d1, at=3, to=x_to)
     send_d2 = link(x2[0], d2, at=4, to=y_to)
     starts = [sum(sizes[:k]) for k in range(count)]
@@ -171,7 +173,9 @@
 
     def forward_top():
         top_recv(y_side, 1)
-        top_d.start()
+        top_d1.start()
+        top_recv(x_side, 0)
+        top_d2.start()
         send_x1[0].start()
         send_y2[0].start()
 
@@ -192,8 +196,9 @@
     state = finish(0, forward_top, queue_rest)
     complete(0, state)
     copies = stage(0)
-    top_recv(x_side, 0)
-    top_recv(3 - c, 2)
+    top_in.wait()
+    for half, at in ((upper, 2), (lower, last_link)):
+        link(top.at[3 - c, half], top.at[3 - c, half], at=at, to=x_to).wait_recv()
     update = rhs[1]
     for q in range(4):
         left = halves(top[q])
@@ -231,7 +236,7 @@
             loads.at[pl.ds(start + 2, size)], partial.at[here])
     for copy in copies:
         copy.wait()
-    for copy in [top_x, top_y, top_d] + send_x1 + send_y1 + send_x2 + send_y2:
+    for copy in [top_x, top_y, top_d1, top_d2] + send_x1 + send_y1 + send_x2 + send_y2:
         copy.wait_send()
     for copy in (send_d1, send_d2):
         copy.wait()
@@ -247,7 +252,7 @@
     shape = jax.ShapeDtypeStruct
     piece = lambda size: shape((size, rows, width), f32)
     pieces = [piece(size) for size in [sum(sizes)] * 2 + [sizes[0]] * 2 + list(sizes) * 2]
-    links = 5 + 4 * len(sizes)
+    links = 6 + 4 * len(sizes)
     sums = 2 * 4 * chips
     return pl.pallas_call(
         functools.partial(solve_kernel, sizes),

time: 413 us -> 413 us (level)
  no operation moved by 1% of the time
where the time goes in v4:
time: 413 us; the launch traced here: 409 us
  Pallas kernels  347 us (84%)
  waiting for transfers between devices  42.7 us (10%)
  other arithmetic  8.53 us (2%)
  starting transfers between devices  8.23 us (2%)
    pallas_call x1, Pallas kernels, solve(): pl.pallas_call(functools.partial(solve_kernel, sizes), out_shape=[shape((...  290 us
    pallas_call x5, Pallas kernels, update_chunk(): pl.pallas_call(functools.partial(update_kernel, len(pieces), step), out_s...  57 us
    ppermute x4, waiting for transfers between devices, local_quarters(): far2[k] = lax.ppermute(near2, 'col', along_y)  23.3 us
    ppermute x4, waiting for transfers between devices, local_quarters(): far1[k] = lax.ppermute(near1, 'col', along_x)  19.5 us
    another operation x1, other arithmetic, local_quarters(): solved, far_high = lax.optimization_barrier((jnp.stack(solved), far_high))  8.53 us
  transfers between devices with their start and end apart: 8, of which 3 were waited for; matrix products, arithmetic and copies ran while one was open for 2% of the time, Pallas kernels for 13%

profile of v4, /device:TPU:16, one launch (start us, length us, event | category | flops | bytes accessed | tf_op | source)
XLA Modules:
  0.0 408.6 jit_solution(14273813100559539778)
XLA Ops:
  0.6 290.2 %shard_map.59 = (f32[1024,1024]{1,0:T(8,128)}, f32[1024,1024]{1,0:T(8,128)}, bf16[2048,1024]{1,0:T(8,128)(2,1)}, bf16[2048,1024]{1,0:T(8,128)(2,1)}, bf16[512,10...) custom-call(f32[48,128,1024]{2,1,0:T(8,128)} %refs_9_.1, ...), custom_call_target="tpu_custom_call" | custom-call | tf_op jit(solution)/shard_map/pallas_call | solution.py:257
  290.8 1.6 collective-permute-start.4
  292.4 0.5 collective-permute-start.6
  292.9 1.5 collective-permute-start
  294.4 0.6 collective-permute-start.2
  295.0 8.5 %pad_maximum_fusion = f32[2,1024,1024]{2,1,0:T(8,128)} fusion(f32[1,1024,1024]{2,1,0:T(8,128)} %bitcast.3, f32[1,1024,1024]{2,1,0:T(8,128)} %bitcast.2), kind=kLoop, calls=%fused_computation | loop fusion | flops 2097152 | bytes 16777216 | tf_op jit(solution)/shard_map/stack | solution.py:354
  303.5 19.4 %collective-permute-done.4.refs_0_ = f32[10,128,256]{2,1,0:T(8,128)} collective-permute-done((f32[10,128,256]{2,1,0:T(8,128)}, f32[10,128,256]{2,1,0:T(8,128)}, u32[]{:S(2)}, u32[]{:S(2)}) %collective-permute-start.4) | collective-permute-done | bytes 1310752 | tf_op jit(solution)/shard_map/ppermute | solution.py:361
  322.9 1.5 collective-permute-done.6.refs_1_
  324.4 0.5 collective-permute-start.7
  324.9 1.5 collective-permute-start.5
  326.4 20.6 %shard_map.60.refs_5_ = f32[46,128,1024]{2,1,0:T(8,128)} custom-call(f32[47,128,256]{2,1,0:T(8,128)} %refs_0_.1, f32[46,128,256]{2,1,0:T(8,128)} %get-tuple-element.56.refs_1_, f32[8,128,256]{2,1,0:T(8,128)} %get-tuple-element.57.refs_2_, f32[8,128,256]{2,1,0:T(8,128)} %get-tuple-element.58.refs_3_, f32[46,128,256]{2,1,0:T(8,128)} %refs_4_.1, ...), custom_call_target="tpu_custom_call" | custom-call | flops 12884901888 | bytes 25165824 | tf_op jit(solution)/shard_map/pallas_call | solution.py:328
  347.0 9.6 %shard_map.61.refs_5_ = f32[46,128,1024]{2,1,0:T(8,128)} custom-call(f32[10,128,256]{2,1,0:T(8,128)} %collective-permute-done.4.refs_0_, f32[10,128,256]{2,1,0:T(8,128)} %collective-permute-done.6.refs_1_, f32[46,128,1024]{2,1,0:T(8,128)} %get-tuple-element.43.refs_2_, bf16[512,1024]{1,0:T(8,128)(2,1)} %get-tuple-element.44.refs_3_, ...), custom_call_target="tpu_custom_call", output_to_operand_aliasing={{}: (5, {})} | custom-call | flops 4026531840 | bytes 15204352 | tf_op jit(solution)/shard_map/pallas_call | solution.py:328
  356.7 0.0 collective-permute-done.refs_0_
  356.7 0.0 copy-start
  356.7 1.3 collective-permute-start.1
  358.0 0.0 collective-permute-done.2.refs_1_
  358.0 0.0 copy-start.1
  358.0 0.8 collective-permute-start.3
  358.8 0.0 copy-done
  358.8 0.4 copy-done.1
  359.2 10.8 %shard_map.62.refs_5_ = f32[46,128,1024]{2,1,0:T(8,128)} custom-call(f32[12,128,256]{2,1,0:T(8,128)} %copy-done, f32[12,128,256]{2,1,0:T(8,128)} %copy-done.1, f32[46,128,1024]{2,1,0:T(8,128)} %get-tuple-element.43.refs_2_, bf16[512,1024]{1,0:T(8,128)(2,1)} %get-tuple-element.44.refs_3_, ...), custom_call_target="tpu_custom_call", output_to_operand_aliasing={{}: (5, {})} | custom-call | flops 4831838208 | bytes 17825792 | tf_op jit(solution)/shard_map/pallas_call | solution.py:328
  370.1 21.8 %collective-permute-done.7.refs_1_ = f32[12,128,256]{2,1,0:T(8,128)} collective-permute-done((f32[12,128,256]{2,1,0:T(8,128)}, f32[12,128,256]{2,1,0:T(8,128)}, u32[]{:S(2)}, u32[]{:S(2)}) %collective-permute-start.7) | collective-permute-done | bytes 1572896 | tf_op jit(solution)/shard_map/ppermute | solution.py:362
  391.8 0.0 collective-permute-done.5.refs_0_
  391.8 10.8 %shard_map.63.refs_5_ = f32[46,128,1024]{2,1,0:T(8,128)} custom-call(f32[12,128,256]{2,1,0:T(8,128)} %collective-permute-done.5.refs_0_, f32[12,128,256]{2,1,0:T(8,128)} %collective-permute-done.7.refs_1_, f32[46,128,1024]{2,1,0:T(8,128)} %get-tuple-element.43.refs_2_, bf16[512,1024]{1,0:T(8,128)(2,1)} %get-tuple-element.44.refs_3_, ...), custom_call_target="tpu_custom_call", output_to_operand_aliasing={{}: (5, {})} | custom-call | flops 4831838208 | bytes 17825792 | tf_op jit(solution)/shard_map/pallas_call | solution.py:328
  402.7 0.0 collective-permute-done.1.refs_0_
  402.7 0.0 copy-start.2
  402.7 0.0 collective-permute-done.3.refs_1_
  402.7 0.8 copy-done.2
  403.5 5.1 %shard_map.64 = f32[46,128,1024]{2,1,0:T(8,128)} custom-call(f32[4,128,256]{2,1,0:T(8,128)} %copy-done.2, f32[4,128,256]{2,1,0:T(8,128)} %collective-permute-done.3.refs_1_, f32[46,128,1024]{2,1,0:T(8,128)} %get-tuple-element.43.refs_2_, bf16[512,1024]{1,0:T(8,128)(2,1)} %get-tuple-element.44.refs_3_, ...), custom_call_target="tpu_custom_call", output_to_operand_aliasing={{}: (5, {})} | custom-call | flops 1610612736 | bytes 7340032 | tf_op jit(solution)/shard_map/pallas_call | solution.py:328
Async XLA Ops:
  290.8 32.1 %collective-permute-start.4 = (f32[10,128,256]{2,1,0:T(8,128)}, f32[10,128,256]{2,1,0:T(8,128)}, u32[]{:S(2)}, u32[]{:S(2)}) collective-permute-start(f32[10,128,256]{2,1,0:T(8,128)} %get-tuple-element.47), channel_id=1, source_target_pairs={{0,1},{1,0},{2,3},{3,2},{4,5},{5,4},{6,7},{7,6},{8,9},{9,8},{10,11... | collective-permute-start | bytes 3932168 | tf_op jit(solution)/shard_map/ppermute | solution.py:361
  292.4 32.0 %collective-permute-start.6 = (f32[10,128,256]{2,1,0:T(8,128)}, f32[10,128,256]{2,1,0:T(8,128)}, u32[]{:S(2)}, u32[]{:S(2)}) collective-permute-start(f32[10,128,256]{2,1,0:T(8,128)} %get-tuple-element.50), channel_id=1, source_target_pairs={{0,2},{1,3},{2,0},{3,1},{4,6},{5,7},{6,4},{7,5},{8,10},{9,11},{10,... | collective-permute-start | bytes 3932168 | tf_op jit(solution)/shard_map/ppermute | solution.py:362
  292.9 63.8 %collective-permute-start = (f32[12,128,256]{2,1,0:T(8,128)}, f32[12,128,256]{2,1,0:T(8,128)S(1)}, u32[]{:S(2)}, u32[]{:S(2)}) collective-permute-start(f32[12,128,256]{2,1,0:T(8,128)} %get-tuple-element.38), channel_id=1, source_target_pairs={{0,1},{1,0},{2,3},{3,2},{4,5},{5,4},{6,7},{7,6},{8,9},{9,8},{10,11... | collective-permute-start | bytes 4718600 | tf_op jit(solution)/shard_map/ppermute | solution.py:361
  294.4 63.6 %collective-permute-start.2 = (f32[12,128,256]{2,1,0:T(8,128)}, f32[12,128,256]{2,1,0:T(8,128)S(1)}, u32[]{:S(2)}, u32[]{:S(2)}) collective-permute-start(f32[12,128,256]{2,1,0:T(8,128)} %get-tuple-element.41), channel_id=1, source_target_pairs={{0,2},{1,3},{2,0},{3,1},{4,6},{5,7},{6,4},{7,5},{8,10},{9,11},{10,... | collective-permute-start | bytes 4718600 | tf_op jit(solution)/shard_map/ppermute | solution.py:362
  324.4 67.4 %collective-permute-start.7 = (f32[12,128,256]{2,1,0:T(8,128)}, f32[12,128,256]{2,1,0:T(8,128)}, u32[]{:S(2)}, u32[]{:S(2)}) collective-permute-start(f32[12,128,256]{2,1,0:T(8,128)} %get-tuple-element.51), channel_id=1, source_target_pairs={{0,2},{1,3},{2,0},{3,1},{4,6},{5,7},{6,4},{7,5},{8,10},{9,11},{10,... | collective-permute-start | bytes 4718600 | tf_op jit(solution)/shard_map/ppermute | solution.py:362
  324.9 66.9 %collective-permute-start.5 = (f32[12,128,256]{2,1,0:T(8,128)}, f32[12,128,256]{2,1,0:T(8,128)}, u32[]{:S(2)}, u32[]{:S(2)}) collective-permute-start(f32[12,128,256]{2,1,0:T(8,128)} %get-tuple-element.48), channel_id=1, source_target_pairs={{0,1},{1,0},{2,3},{3,2},{4,5},{5,4},{6,7},{7,6},{8,9},{9,8},{10,11... | collective-permute-start | bytes 4718600 | tf_op jit(solution)/shard_map/ppermute | solution.py:361
  356.7 2.1 copy-start
  356.7 46.0 %collective-permute-start.1 = (f32[4,128,256]{2,1,0:T(8,128)}, f32[4,128,256]{2,1,0:T(8,128)S(1)}, u32[]{:S(2)}, u32[]{:S(2)}) collective-permute-start(f32[4,128,256]{2,1,0:T(8,128)} %get-tuple-element.39), channel_id=1, source_target_pairs={{0,1},{1,0},{2,3},{3,2},{4,5},{5,4},{6,7},{7,6},{8,9},{9,8},{10,11... | collective-permute-start | bytes 1572872 | tf_op jit(solution)/shard_map/ppermute | solution.py:361
  358.0 1.2 copy-start.1
  358.0 44.7 %collective-permute-start.3 = (f32[4,128,256]{2,1,0:T(8,128)}, f32[4,128,256]{2,1,0:T(8,128)}, u32[]{:S(2)}, u32[]{:S(2)}) collective-permute-start(f32[4,128,256]{2,1,0:T(8,128)} %get-tuple-element.42), channel_id=1, source_target_pairs={{0,2},{1,3},{2,0},{3,1},{4,6},{5,7},{6,4},{7,5},{8,10},{9,11},{10,... | collective-permute-start | bytes 1572872 | tf_op jit(solution)/shard_map/ppermute | solution.py:362
  402.7 0.8 copy-start.2
